TPU v7x, 1024 devices: a whole 4x8x16 slice. The times are simulated.
1024 devices in a mesh: row: 16 (over y, core), col: 64 (over z, x).
Axes of the slice: x: 4, y: 8, z: 16, core: 2. Of those that a mesh axis runs over, the one named last changes fastest.
Arguments:
- tangent: bfloat16 [16, 64, 64, 4096], P('row', 'col')
- block_row: int32 [16, 64, 64], P('row', 'col'), may hold values from 0 to 127
- block_col: int32 [16, 64, 64], P('row', 'col'), may hold values from 0 to 31
- tile_count: int32 [16, 64], P('row', 'col'), may hold values from 1 to 64, 2560 in all within a row
- old_basis: bfloat16 [2048, 3072], P(('row', 'col'))
- old_id: int32 [2048], P(('row', 'col')), may hold values from 0 to 2047, as said below
- residual: float32 [131072], P(('row', 'col'))
Outputs:
- recycled_c: bfloat16 [2048, 3072], P(('row', 'col'))
- recycled_u: bfloat16 [2048, 3072], P(('row', 'col'))
- coefficients: float32 [48], replicated
Inputs may be any that keep to these rules, and one draw needn't show every extreme that they name: old_id is a permutation of the block rows. Write slot s = (128 * r + 2 * c + i) with 0 <= c < 64 and 0 <= i < 2, and p = i // 2. Its new block row is 128 * r + 2 * ((c + p + 1) mod (64)) + 2 * p + e, with e 0 or 1, the two slots of a pair taking different e. In each row of tile_count the largest count is exactly 64.
All inputs are finite; a program needn't handle non-finite values. No bound on the sum of `tile_count` on one device may be relied on, other than what follows from the above.
Results may differ from a plain program's by a relative error of at most 0.0012.
Values may be sent and summed in bfloat16 or wider, within the bound.
No kernel may reach another device: no remote copies, remote signals or barrier semaphores. Data moves between devices by JAX's collectives and lax.ppermute only.
A program may use at most 32 MiB of HBM per device.

v0:
```python
import math

import jax
import jax.numpy as jnp
from jax import lax
from jax.sharding import PartitionSpec as P

BLK = 64
K = 48


def passed_along(array, axis, by):
    peers = lax.axis_size(axis)
    return lax.ppermute(array, axis, [(i, (i + by) % peers) for i in range(peers)])


def per_device(tangent, block_row, block_col, tile_count, old_basis, old_id, residual):
    highest = lax.Precision.HIGHEST
    per_dev = old_basis.shape[0]
    col_count = lax.axis_size("col")
    row_count = lax.axis_size("row")
    new_slot = old_id % per_dev
    labels = (new_slot - 0 + 1).astype(jnp.bfloat16)
    incoming, in_labels = passed_along((old_basis, labels), "col", 1)
    wanted = jnp.arange(1, 3, dtype=jnp.float32)
    placing = (in_labels.astype(jnp.float32)[None, :] == wanted[:, None]).astype(jnp.bfloat16)
    placed = jnp.dot(placing, incoming, preferred_element_type=jnp.float32).astype(jnp.bfloat16)
    col_basis = lax.all_gather(placed, "row", axis=0, tiled=True)
    values = tangent[0, 0]
    rows_local = block_row[0, 0]
    cols_local = block_col[0, 0]
    live_count = tile_count[0, 0]
    stored = values.shape[0]
    group = min(128, stored)
    tile_rows = per_dev * col_count

    def add_group(index, partial_value):
        start = index * group
        block_vals = values.reshape(group, BLK, BLK)
        picked = col_basis[cols_local].reshape(group, BLK, K)
        prods = jnp.einsum("gij,gjk->gik", block_vals, picked, preferred_element_type=jnp.float32)
        alive = start + jnp.arange(group, dtype=jnp.int32) < live_count
        prods = jnp.where(alive[:, None, None], prods, jnp.float32(0.0)).reshape(group, BLK * K)
        return partial_value.at[rows_local].add(prods)

    trips = (live_count + group - 1) // group
    partial_value = lax.fori_loop(0, trips, add_group, jnp.zeros((tile_rows, BLK * K), jnp.float32))
    product = lax.psum_scatter(partial_value, "col", scatter_dimension=0, tiled=True)
    flat_c = product.reshape(per_dev * BLK, K)
    total_rows = per_dev * row_count * col_count * BLK
    gram_part = jnp.dot(flat_c.T, flat_c, precision=highest)
    gram = lax.psum(gram_part, ("row", "col"))
    lower = jnp.linalg.cholesky(gram / jnp.float32(total_rows))
    ortho_t = jax.scipy.linalg.solve_triangular(lower, flat_c.T, lower=True)
    inner = lax.psum(jnp.dot(ortho_t, residual, precision=highest), ("row", "col"))
    coefficients = inner / jnp.float32(math.sqrt(total_rows))
    basis_t = jax.scipy.linalg.solve_triangular(
        lower, placed.astype(jnp.float32).reshape(per_dev * BLK, K).T, lower=True
    )
    recycled_c = ortho_t.T.reshape(per_dev, BLK * K).astype(jnp.bfloat16)
    recycled_u = basis_t.T.reshape(per_dev, BLK * K).astype(jnp.bfloat16)
    return (recycled_c, recycled_u, coefficients)


def solution(mesh):
    return jax.shard_map(
        per_device,
        mesh=mesh,
        in_specs=(
            P("row", "col", None, None),
            P("row", "col", None),
            P("row", "col", None),
            P("row", "col"),
            P(("row", "col"), None),
            P(("row", "col")),
            P(("row", "col")),
        ),
        out_specs=(P(("row", "col"), None), P(("row", "col"), None), P()),
        check_vma=False,
    )
```

profile of v0, /device:TPU:1, one launch (start us, length us, event | category | flops | bytes accessed | tf_op | source)
XLA Modules:
  0.0 604.4 jit_solution(5229694401126696101)
XLA Ops:
  7.2 0.0 copy-start
  7.2 0.0 copy-start.2
  7.2 0.0 copy-start.3
  7.2 0.0 all-reduce.3.cloned.1.call-start
  7.2 3.9 collective-permute-start.1
  11.2 0.7 fusion.12
  11.9 3.1 collective-permute-start
  15.7 16.1 %collective-permute-done = bf16[2]{0:T(256)(128)(2,1)S(1)} collective-permute-done((bf16[2]{0:T(256)(128)(2,1)S(1)}, bf16[2]{0:T(256)(128)(2,1)S(1)}, u32[]{:S(2)}, u32[]{:S(2)}) %collective-permute-start) | collective-permute-done | bytes 36 | tf_op jit(solution)/shard_map/ppermute | solution.py:14
  31.7 0.0 collective-permute-done.1
  31.7 0.2 convolution_convert_fusion
  31.9 19.5 %all-gather = bf16[16,2,3072]{2,1,0:T(2,128)(2,1)S(1)} all-gather(bf16[1,2,3072]{2,1,0:T(2,128)(2,1)S(1)} %bitcast.62), channel_id=1, replica_groups=mesh['row'=16,'col'=64] {'row'}, dimensions={0}, use_global_device_ids=true | all-gather | bytes 208896 | tf_op jit(solution)/shard_map/all_gather | solution.py:28
  51.4 0.1 reshape.92
  51.5 0.1 broadcast_in_dim.22
  51.7 0.0 copy-done.2
  51.7 0.0 copy-done.3
  51.7 15.5 %while.10 = (s32[]{:T(128)}, f32[128,3072]{1,0:T(8,128)S(1)}, s32[]{:T(128)}, s32[64]{0:T(128)S(1)}, s32[]{:T(128)}, /*index=5*/s32[64]{0:T(128)S(1)}, bf16[32,3...) while((s32[]{:T(128)}, f32[128,3072]{1,0:T(8,128)S(1)}, s32[]{:T(128)}, ...), condition=%wide.region_2.3_spmd, body=%wide.region_0.2_spmd.sunk | while | flops 25560580 | bytes 9836545 | solution.py:47
  51.7 0.8 gather_fusion
  52.5 2.1 reshape.106
  54.6 2.8 reshape_squeeze.4
  57.4 0.7 add_compare_fusion.2
  58.0 2.3 select_bitcast_fusion.2
  60.3 1.9 copy.28
  62.2 2.8 reshape.107
  65.0 2.2 scatter_fusion
  67.2 0.0 copy-start.1
  67.2 1.1 copy-done.1
  68.4 0.0 all-reduce.3.cloned.1.call-update
  68.4 1.3 dynamic-slice
  70.3 0.1 reshape.74
  70.4 268.9 %all-reduce.3.cloned.1.call-done = f32[128,3072]{1,0:T(8,128)} async-done(((f32[128,3072]{1,0:T(8,128)}), f32[128,3072]{1,0:T(8,128)}) %all-reduce.3.cloned.1.call-update) | async-done | bytes 1572880
  339.3 0.9 constant_dynamic-slice_fusion
  340.2 0.1 reshape.72
  340.3 0.3 fusion.17
  340.6 127.3 %psum.14 = f32[48,48]{0,1:T(8,128)S(1)} all-reduce(f32[48,48]{0,1:T(8,128)S(1)} %fusion.17), channel_id=1, replica_groups=mesh['row'=16,'col'=64] {'row','col'}, use_global_device_ids=true, to_apply=%region_4.5 | all-reduce | flops 2304 | bytes 18432 | tf_op jit(solution)/shard_map/psum | solution.py:52
  467.9 0.1 copy.22
  468.0 4.4 cholesky.18
  472.4 0.6 compare_reduce_fusion
  473.1 0.7 fusion.6
  473.7 3.7 custom-call.7
  477.4 0.3 fusion.4
  477.7 0.1 copy.23
  477.8 0.7 convert_element_type.34
  478.6 0.3 fusion.2
  478.8 0.1 copy.24
  478.9 0.7 convert_element_type.37
  479.7 0.0 copy-done
  479.7 0.1 convolution_bitcast_fusion
  479.8 117.2 %psum.15 = f32[48]{0:T(128)S(1)} all-reduce(f32[48]{0:T(128)S(1)} %convolution_bitcast_fusion), channel_id=1, replica_groups=mesh['row'=16,'col'=64] {'row','col'}, use_global_device_ids=true, to_apply=%region_7.9 | all-reduce | flops 48 | bytes 384 | tf_op jit(solution)/shard_map/psum | solution.py:55
  597.0 0.5 broadcast_multiply_fusion.1
  (8 shorter events, 0.1 us)
Async XLA Ops:
  7.2 472.5 %copy-start = (f32[128]{0:T(128)S(1)}, f32[128]{0:T(128)}, u32[]{:S(2)}) copy-start(f32[128]{0:T(128)} %param.17) | copy-start | bytes 1540
  7.2 44.5 %copy-start.2 = (s32[1,1,64]{2,1,0:T(1,128)S(1)}, s32[1,1,64]{2,1,0:T(1,128)}, u32[]{:S(2)}) copy-start(s32[1,1,64]{2,1,0:T(1,128)} %param.12) | copy-start | bytes 772
  7.2 44.5 %copy-start.3 = (s32[1,1,64]{2,1,0:T(1,128)S(1)}, s32[1,1,64]{2,1,0:T(1,128)}, u32[]{:S(2)}) copy-start(s32[1,1,64]{2,1,0:T(1,128)} %param.13) | copy-start | bytes 772
  7.2 332.1 %all-reduce.3.cloned.1.call-start = ((), (), s32[]{:S(2)}) async-start(), calls=%async_computation | async-start | bytes 3145728
  7.2 24.5 %collective-permute-start.1 = (bf16[2,3072]{1,0:T(2,128)(2,1)}, bf16[2,3072]{1,0:T(2,128)(2,1)S(1)}, u32[]{:S(2)}, u32[]{:S(2)}) collective-permute-start(bf16[2,3072]{1,0:T(2,128)(2,1)} %param.15), channel_id=1, source_target_pairs={{0,1},{1,2},{2,3},{3,4},{4,5},{5,6},{6,7},{7,8},{8,9},{9,10},{10,1... | collective-permute-start | bytes 36872 | tf_op jit(solution)/shard_map/ppermute | solution.py:14
  11.9 19.9 %collective-permute-start = (bf16[2]{0:T(256)(128)(2,1)S(1)}, bf16[2]{0:T(256)(128)(2,1)S(1)}, u32[]{:S(2)}, u32[]{:S(2)}) collective-permute-start(bf16[2]{0:T(256)(128)(2,1)S(1)} %fusion.12), channel_id=1, source_target_pairs={{0,1},{1,2},{2,3},{3,4},{4,5},{5,6},{6,7},{7,8},{8,9},{9,10},{10,1... | collective-permute-start | bytes 20 | tf_op jit(solution)/shard_map/ppermute | solution.py:14
  67.2 1.1 copy-start.1
Sparse Core Ops, SparseCore 0:
  68.5 270.7 all-reduce.2
where the time goes:
time: 605 us; the launch traced here: 604 us
  waiting for transfers between devices  285 us (47%)
  blocking collectives  264 us (44%)
  local copies, waits for them, and re-layouts  15.9 us (3%)
  between operations  15.5 us (3%)
  other arithmetic  13.4 us (2%)
  starting transfers between devices  7.09 us (1%)
    unnamed x2, waiting for transfers between devices  269 us
    psum x1, blocking collectives, per_device(): gram = lax.psum(gram_part, ('row', 'col'))  127 us
    psum x1, blocking collectives, per_device(): lax.psum(jnp.dot(ortho_t, residual, precision=highest), ('row', 'col'))  117 us
    all_gather x1, blocking collectives, per_device(): col_basis = lax.all_gather(placed, 'row', axis=0, tiled=True)  19.5 us
    ppermute x2, waiting for transfers between devices, passed_along(): lax.ppermute(array, axis, [(i, (i + by) % peers) for i in range(peers)])  16.1 us
  transfers between devices with their start and end apart: 3, of which 2 were waited for; matrix products, arithmetic and copies ran while one was open for 0% of the time, Pallas kernels for 0%

commit v1 on v0

v1 whole, which is shorter than its diff:
```python
import math

import jax
import jax.numpy as jnp
from jax import lax
from jax.experimental import pallas as pl
from jax.experimental.pallas import tpu as pltpu
from jax.sharding import Mesh
from jax.sharding import PartitionSpec as P

BLK = 64
K = 48
PAIR = 2 * BLK
N_X, N_Y, N_Z, N_CORE = 4, 8, 16, 2
ROW = ("y", "core")
COL = ("z", "x")
N_ROW = N_Y * N_CORE
N_COL = N_Z * N_X
NNZ = 64
TOTAL = N_ROW * N_COL * PAIR
HIGHEST = lax.Precision.HIGHEST
VMEM = 48 * 1024 * 1024


def product_kernel(row_ref, col_ref, count_ref, tangent_ref, basis_ref, out_ref, half_ref):
    for q in range(N_ROW):
        half_ref[2 * q] = basis_ref[q, :, :BLK]
        half_ref[2 * q + 1] = basis_ref[q, :, BLK:]
    out_ref[...] = jnp.zeros_like(out_ref)
    count = count_ref[0]

    def add_block(n, carry):
        row = row_ref[n]
        owner = row >> 1
        place = (owner & (N_X - 1)) * N_Z + (owner >> 2)
        side = jnp.where(n < count, row & 1, 2)
        block = tangent_ref[n]
        none = jnp.zeros_like(block)
        sides = jnp.concatenate([jnp.where(side == 0, block, none), jnp.where(side == 1, block, none)], axis=0)
        out_ref[place] += lax.dot_general(
            half_ref[col_ref[n]], sides, (((1,), (1,)), ((), ())), preferred_element_type=jnp.float32
        )
        return carry

    lax.fori_loop(0, NNZ, add_block, 0, unroll=8)


def gram_kernel(parts_ref, residual_ref, product_ref, gram_ref):
    product = jnp.sum(parts_ref[...], axis=0)
    product_ref[...] = product
    first = lax.broadcasted_iota(jnp.int32, (16, PAIR), 0) == 0
    extra = jnp.where(first, jnp.broadcast_to(residual_ref[...], (16, PAIR)), 0.0)
    both = jnp.concatenate([product, extra], axis=0)
    gram = lax.dot_general(product, both, (((1,), (1,)), ((), ())), precision=HIGHEST)
    gram_ref[...] = jnp.concatenate([gram[: K // 2], gram[K // 2 :]], axis=1)


def finish_kernel(gram_ref, product_ref, basis_ref, out_c_ref, out_u_ref, coeff_ref):
    packed = gram_ref[...]
    upper = jnp.concatenate([packed[:, :BLK], packed[:, BLK:]], axis=0)
    work = jnp.concatenate([upper, jnp.zeros_like(upper)], axis=1)
    at_row = lax.broadcasted_iota(jnp.int32, (K, PAIR), 0)
    at_lane = lax.broadcasted_iota(jnp.int32, (K, PAIR), 1)
    work = jnp.where(at_lane < K, work * (1.0 / TOTAL), work)
    work = jnp.where(at_lane == at_row + BLK, 1.0, work)
    for k in range(K - 1):
        pivot_row = work[k : k + 1, :]
        factor = work[:, k : k + 1] / pivot_row[:, k : k + 1]
        work = work - jnp.where(at_row > k, factor * pivot_row, 0.0)
    pivots = jnp.sum(jnp.where(at_lane == at_row, work, 0.0), axis=1, keepdims=True)
    work = work / jnp.sqrt(pivots)
    inverse = jnp.where(at_lane >= BLK, work, 0.0)

    def transformed(columns):
        tall = jnp.concatenate(
            [jnp.zeros((BLK, PAIR), jnp.float32), columns, jnp.zeros((BLK - K, PAIR), jnp.float32)], axis=0
        )
        return jnp.dot(inverse, tall, precision=HIGHEST).T.astype(jnp.bfloat16)

    out_c_ref[...] = transformed(product_ref[...])
    out_u_ref[...] = transformed(basis_ref[...].astype(jnp.float32))
    inner = work[:, K : K + 1] * (1.0 / math.sqrt(TOTAL))
    coeff_ref[...] = jnp.sum(jnp.where(at_lane == at_row, inner, 0.0), axis=0, keepdims=True)


def summed(array, axes, count):
    copies = jnp.broadcast_to(array[None], (count,) + array.shape)
    return jnp.sum(lax.all_to_all(copies, axes, 0, 0, tiled=True), axis=0)


def per_device(tangent, block_row, block_col, tile_count, old_basis, old_id, residual):
    params = pltpu.CompilerParams(vmem_limit_bytes=VMEM)
    smem = pl.BlockSpec(memory_space=pltpu.SMEM)
    vmem = pl.BlockSpec(memory_space=pltpu.VMEM)
    ordered = jnp.where(old_id[0] % 2 == 0, old_basis, old_basis[::-1])
    sideways = ordered.reshape(2, BLK, K).transpose(2, 0, 1).reshape(K, PAIR)
    placed = lax.ppermute(sideways, COL, [(i, (i + 1) % N_COL) for i in range(N_COL)])
    copies = jnp.broadcast_to(placed[None], (N_ROW, K, PAIR))
    col_basis = lax.all_to_all(copies, ROW, 0, 0, tiled=True)
    partial = pl.pallas_call(
        product_kernel,
        out_shape=jax.ShapeDtypeStruct((N_COL, K, PAIR), jnp.float32),
        in_specs=[smem, smem, smem, vmem, vmem],
        out_specs=vmem,
        scratch_shapes=[pltpu.VMEM((2 * N_ROW, K, BLK), jnp.bfloat16)],
        compiler_params=params,
    )(block_row.reshape(NNZ), block_col.reshape(NNZ), tile_count.reshape(1), tangent.reshape(NNZ, BLK, BLK), col_basis)
    over_x = lax.all_to_all(partial, "x", 0, 0, tiled=True)
    over_x = jnp.sum(over_x.reshape(N_X, N_Z, K, PAIR), axis=0)
    over_z = lax.all_to_all(over_x, "z", 0, 0, tiled=True)
    product, gram = pl.pallas_call(
        gram_kernel,
        out_shape=(
            jax.ShapeDtypeStruct((K, PAIR), jnp.float32),
            jax.ShapeDtypeStruct((K // 2, PAIR), jnp.float32),
        ),
        in_specs=[vmem, vmem],
        out_specs=(vmem, vmem),
        compiler_params=params,
    )(over_z, residual.reshape(1, PAIR))
    gram = summed(gram, "x", N_X)
    gram = summed(gram, ROW, N_ROW)
    gram = summed(gram, "z", N_Z)
    out_c, out_u, coefficients = pl.pallas_call(
        finish_kernel,
        out_shape=(
            jax.ShapeDtypeStruct((PAIR, K), jnp.bfloat16),
            jax.ShapeDtypeStruct((PAIR, K), jnp.bfloat16),
            jax.ShapeDtypeStruct((1, PAIR), jnp.float32),
        ),
        in_specs=[vmem, vmem, vmem],
        out_specs=(vmem, vmem, vmem),
        compiler_params=params,
    )(gram, product, placed)
    return (out_c.reshape(2, BLK * K), out_u.reshape(2, BLK * K), coefficients[0, :K])


def solution(mesh):
    split = Mesh(mesh.devices.reshape(N_Y, N_CORE, N_Z, N_X), ("y", "core", "z", "x"))
    return jax.shard_map(
        per_device,
        mesh=split,
        in_specs=(
            P(ROW, COL, None, None),
            P(ROW, COL, None),
            P(ROW, COL, None),
            P(ROW, COL),
            P(ROW + COL, None),
            P(ROW + COL),
            P(ROW + COL),
        ),
        out_specs=(P(ROW + COL, None), P(ROW + COL, None), P()),
        check_vma=False,
    )
```

time: 605 us -> 159 us (0.26)
  waiting for transfers between devices: 285 us -> 25.7 us
  blocking collectives: 264 us -> 93.8 us
  other arithmetic: 13.4 us -> 0.9 us
  between operations: 15.5 us -> 3.34 us
  Pallas kernels: 0 us -> 7.64 us
    unnamed x2 -> x0, waiting for transfers between devices: 269 us -> none
    psum x2 -> x0, blocking collectives: 245 us -> none  [the longest x1 127 us: per_device(): gram = lax.psum(gram_part, ('row', 'col'))]
    all_to_all x0 -> x5, blocking collectives: none -> 93.8 us  [the longest x3 46.5 us: summed(): return jnp.sum(lax.all_to_all(copies, axes, 0, 0, tiled=True), axis=0)]
    all_gather x1 -> x0, blocking collectives: 19.5 us -> none  [per_device(): col_basis = lax.all_gather(placed, 'row', axis=0, tiled=True)]
    another operation x5 -> x0, other arithmetic: 9.38 us -> none  [the longest x3 5.05 us: per_device(): lower = jnp.linalg.cholesky(gram / jnp.float32(total_rows))]
    rev x0 -> x1, local copies, waits for them, and re-layouts: none -> 8.16 us  [per_device(): ordered = jnp.where(old_id[0] % 2 == 0, old_basis, old_basis[::-1])]
    all_to_all x0 -> x1, starting transfers between devices: none -> 7.96 us  [per_device(): col_basis = lax.all_to_all(copies, ROW, 0, 0, tiled=True)]
    pallas_call x0 -> x3, Pallas kernels: none -> 7.64 us  [the longest x1 4.24 us: per_device(): pl.pallas_call(finish_kernel, out_shape=(jax.ShapeDtypeStruct((PAIR, K),...]
  transfers between devices with their start and end apart: 3 -> 2, of which waited for: 2 -> 2; matrix products, arithmetic and copies ran while one was open for 0% -> 1% of each run, Pallas kernels for 0% -> 0%
where the time goes in v1:
time: 159 us; the launch traced here: 156 us
  blocking collectives  93.8 us (59%)
  waiting for transfers between devices  25.7 us (16%)
  local copies, waits for them, and re-layouts  13.1 us (8%)
  starting transfers between devices  11.9 us (7%)
  Pallas kernels  7.64 us (5%)
  between operations  3.34 us (2%)
    all_to_all x3, blocking collectives, summed(): return jnp.sum(lax.all_to_all(copies, axes, 0, 0, tiled=True), axis=0)  46.5 us
    all_to_all x1, blocking collectives, per_device(): over_z = lax.all_to_all(over_x, 'z', 0, 0, tiled=True)  23.7 us
    all_to_all x1, blocking collectives, per_device(): over_x = lax.all_to_all(partial, 'x', 0, 0, tiled=True)  23.5 us
    ppermute x1, waiting for transfers between devices, per_device(): lax.ppermute(sideways, COL, [(i, (i + 1) % N_COL) for i in range(N_COL)])  18.1 us
    rev x1, local copies, waits for them, and re-layouts, per_device(): ordered = jnp.where(old_id[0] % 2 == 0, old_basis, old_basis[::-1])  8.16 us
    all_to_all x1, starting transfers between devices, per_device(): col_basis = lax.all_to_all(copies, ROW, 0, 0, tiled=True)  7.96 us
    all_to_all x1, waiting for transfers between devices, per_device(): col_basis = lax.all_to_all(copies, ROW, 0, 0, tiled=True)  7.61 us
    pallas_call x1, Pallas kernels, per_device(): pl.pallas_call(finish_kernel, out_shape=(jax.ShapeDtypeStruct((PAIR, K),...  4.24 us
  transfers between devices with their start and end apart: 2, of which 2 were waited for; matrix products, arithmetic and copies ran while one was open for 1% of the time, Pallas kernels for 0%

profile of v1, /device:TPU:1, one launch (start us, length us, event | category | flops | bytes accessed | tf_op | source)
XLA Modules:
  0.0 156.4 jit_solution(17576666979704608092)
XLA Ops:
  0.6 0.0 copy-start.2
  0.6 0.0 copy-start.1
  2.6 8.2 %rev.3 = bf16[2,3072]{1,0:T(2,128)(2,1)S(1)} reverse(bf16[2,3072]{1,0:T(2,128)(2,1)} %param.11), dimensions={0} | reverse | bytes 24576 | tf_op jit(solution)/shard_map/rev | solution.py:95
  10.8 0.7 broadcast_select_fusion
  11.5 0.1 reshape.44
  11.6 0.1 copy.13
  11.7 4.0 %collective-permute-start = (bf16[48,128]{1,0:T(8,128)(2,1)S(1)}, bf16[48,128]{1,0:T(8,128)(2,1)S(1)}, u32[]{:S(2)}, u32[]{:S(2)}) collective-permute-start(bf16[48,128]{1,0:T(8,128)(2,1)S(1)} %copy.13), channel_id=1, source_target_pairs={{0,1},{1,2},{2,3},{3,4},{4,5},{5,6},{6,7},{7,8},{8,9},{9,10},{10,1... | collective-permute-start | bytes 36872 | tf_op jit(solution)/shard_map/ppermute | solution.py:97
  15.7 18.1 %collective-permute-done.basis_ref = bf16[48,128]{1,0:T(8,128)(2,1)S(1)} collective-permute-done((bf16[48,128]{1,0:T(8,128)(2,1)S(1)}, bf16[48,128]{1,0:T(8,128)(2,1)S(1)}, u32[]{:S(2)}, u32[]{:S(2)}) %collective-permute-start) | collective-permute-done | bytes 12320 | tf_op jit(solution)/shard_map/ppermute | solution.py:97
  33.8 0.7 broadcast_in_dim.8
  34.4 8.0 %all-to-all-start = ((bf16[16,48,128]{2,1,0:T(8,128)(2,1)}), bf16[16,48,128]{2,1,0:T(8,128)(2,1)S(1)}, u32[]{:S(2)}, u32[]{:S(2)}) async-start(bf16[16,48,128]{2,1,0:T(8,128)(2,1)} %broadcast_in_dim.8), calls=%async_computation | async-start | bytes 393216 | tf_op jit(solution)/shard_map/all_to_all | solution.py:99
  43.1 2.1 %reshape.43.tangent_ref = bf16[64,64,64]{2,1,0:T(8,128)(2,1)S(1)} reshape(bf16[1,1,64,4096]{3,2,1,0:T(8,128)(2,1)} %param.7) | data formatting | bytes 1048576 | tf_op jit(solution)/shard_map/reshape | solution.py:107
  45.1 7.6 %all-to-all-done.basis_ref = bf16[16,48,128]{2,1,0:T(8,128)(2,1)S(1)} async-done(((bf16[16,48,128]{2,1,0:T(8,128)(2,1)}), bf16[16,48,128]{2,1,0:T(8,128)(2,1)S(1)}, u32[]{:S(2)}, u32[]{:S(2)}) %all-to-all-start) | async-done | bytes 196640 | tf_op jit(solution)/shard_map/all_to_all | solution.py:99
  52.7 0.0 copy-done.2
  52.7 0.0 copy-done.1
  52.7 3.2 %shard_map.94 = f32[64,48,128]{2,1,0:T(8,128)S(1)} custom-call(s32[64]{0:T(128)S(1)} %bitcast.16, s32[64]{0:T(128)S(1)} %bitcast.17, s32[1]{0:T(128)} %bitcast.14.count_ref, bf16[64,64,64]{2,1,0:T(8,128)(2,1)S(1)} %reshape.43.tangent_ref, bf16[16,48,128]{2,1,0:T(8,128)(2,1)S(1)} %all-to-all-done.basis_ref), custom_call_target="tpu_custom_call" | custom-call | tf_op jit(solution)/shard_map/pallas_call | solution.py:100
  55.9 23.5 %all_to_all.30 = f32[64,48,128]{2,1,0:T(8,128)S(1)} all-to-all(f32[64,48,128]{2,1,0:T(8,128)S(1)} %shard_map.94), channel_id=1, replica_groups=mesh['y'=8,'core'=2,'z'=16,'x'=4] {'x'}, dimensions={0} | all-to-all | bytes 3145728 | tf_op jit(solution)/shard_map/all_to_all | solution.py:108
  79.4 0.0 copy-start
  79.4 0.1 reduce_sum.36
  79.6 23.7 %all_to_all.31.parts_ref = f32[16,48,128]{2,1,0:T(8,128)S(1)} all-to-all(f32[16,48,128]{2,1,0:T(8,128)S(1)} %reduce_sum.36), channel_id=1, replica_groups=mesh['y'=8,'core'=2,'z'=16,'x'=4] {'z'}, dimensions={0} | all-to-all | bytes 786432 | tf_op jit(solution)/shard_map/all_to_all | solution.py:110
  103.3 0.0 copy-done
  103.3 0.2 shard_map.95
  103.5 6.8 %all_to_all.32 = f32[4,24,128]{2,1,0:T(8,128)S(1)} all-to-all(f32[4,24,128]{2,1,0:T(8,128)S(1)} %broadcast_in_dim.9), channel_id=1, replica_groups=mesh['y'=8,'core'=2,'z'=16,'x'=4] {'x'}, dimensions={0} | all-to-all | bytes 98304 | tf_op jit(solution)/shard_map/all_to_all | solution.py:88
  110.3 20.9 %all_to_all.33 = f32[16,24,128]{2,1,0:T(8,128)S(1)} all-to-all(f32[16,24,128]{2,1,0:T(8,128)S(1)} %broadcast_in_dim.10), channel_id=1, replica_groups=mesh['y'=8,'core'=2,'z'=16,'x'=4] {'y','core'}, dimensions={0} | all-to-all | bytes 393216 | tf_op jit(solution)/shard_map/all_to_all | solution.py:88
  131.3 18.9 %all_to_all.34 = f32[16,24,128]{2,1,0:T(8,128)S(1)} all-to-all(f32[16,24,128]{2,1,0:T(8,128)S(1)} %broadcast_in_dim.11), channel_id=1, replica_groups=mesh['y'=8,'core'=2,'z'=16,'x'=4] {'z'}, dimensions={0} | all-to-all | bytes 393216 | tf_op jit(solution)/shard_map/all_to_all | solution.py:88
  150.2 4.2 %shard_map.96 = (bf16[128,48]{1,0:T(8,128)(2,1)S(1)}, bf16[128,48]{1,0:T(8,128)(2,1)S(1)}, f32[1,128]{1,0:T(1,128)S(1)}) custom-call(f32[24,128]{1,0:T(8,128)S(1)} %reduce_sum.39.gram_ref, f32[48,128]{1,0:T(8,128)S(1)} %get-tuple-element.9.product_ref, bf16[48,128]{1,0:T(8,128)(2,1)S(1)} %collective-permute-done.basis_ref), custom_call_target="tpu_custom_call" | custom-call | tf_op jit(solution)/shard_map/pallas_call | solution.py:124
  154.4 0.7 reshape.48
  155.1 0.5 slice_bitcast_fusion
  155.7 0.7 reshape.49
  (6 shorter events, 0.1 us)
Async XLA Ops:
  0.6 52.1 %copy-start.2 = (s32[1,1,64]{2,1,0:T(1,128)S(1)}, s32[1,1,64]{2,1,0:T(1,128)}, u32[]{:S(2)}) copy-start(s32[1,1,64]{2,1,0:T(1,128)} %param.9) | copy-start | bytes 772
  0.6 52.1 %copy-start.1 = (s32[1,1,64]{2,1,0:T(1,128)S(1)}, s32[1,1,64]{2,1,0:T(1,128)}, u32[]{:S(2)}) copy-start(s32[1,1,64]{2,1,0:T(1,128)} %param.8) | copy-start | bytes 772
  11.7 22.1 %collective-permute-start = (bf16[48,128]{1,0:T(8,128)(2,1)S(1)}, bf16[48,128]{1,0:T(8,128)(2,1)S(1)}, u32[]{:S(2)}, u32[]{:S(2)}) collective-permute-start(bf16[48,128]{1,0:T(8,128)(2,1)S(1)} %copy.13), channel_id=1, source_target_pairs={{0,1},{1,2},{2,3},{3,4},{4,5},{5,6},{6,7},{7,8},{8,9},{9,10},{10,1... | collective-permute-start | bytes 36872 | tf_op jit(solution)/shard_map/ppermute | solution.py:97
  34.4 18.3 %all-to-all-start = ((bf16[16,48,128]{2,1,0:T(8,128)(2,1)}), bf16[16,48,128]{2,1,0:T(8,128)(2,1)S(1)}, u32[]{:S(2)}, u32[]{:S(2)}) async-start(bf16[16,48,128]{2,1,0:T(8,128)(2,1)} %broadcast_in_dim.8), calls=%async_computation | async-start | bytes 393216 | tf_op jit(solution)/shard_map/all_to_all | solution.py:99
  79.4 23.9 %copy-start = (f32[128]{0:T(128)S(1)}, f32[128]{0:T(128)}, u32[]{:S(2)}) copy-start(f32[128]{0:T(128)} %param.13) | copy-start | bytes 1540

commit v2 on v1

--- a/solution.py
+++ b/solution.py
@@ -11,11 +11,14 @@
 BLK = 64
 K = 48
 PAIR = 2 * BLK
-N_X, N_Y, N_Z, N_CORE = 4, 8, 16, 2
+N_X, N_Y, N_CORE = 4, 8, 2
+N_Z_HI, N_Z_LO = 8, 2
 ROW = ("y", "core")
-COL = ("z", "x")
+NEAR = ("z_lo", "x")
+COL = ("z_hi",) + NEAR
 N_ROW = N_Y * N_CORE
-N_COL = N_Z * N_X
+N_NEAR = N_Z_LO * N_X
+N_COL = N_Z_HI * N_NEAR
 NNZ = 64
 TOTAL = N_ROW * N_COL * PAIR
 HIGHEST = lax.Precision.HIGHEST
@@ -32,7 +35,7 @@
     def add_block(n, carry):
         row = row_ref[n]
         owner = row >> 1
-        place = (owner & (N_X - 1)) * N_Z + (owner >> 2)
+        place = (owner & (N_NEAR - 1)) * N_Z_HI + (owner >> 3)
         side = jnp.where(n < count, row & 1, 2)
         block = tangent_ref[n]
         none = jnp.zeros_like(block)
@@ -80,7 +83,7 @@
     out_c_ref[...] = transformed(product_ref[...])
     out_u_ref[...] = transformed(basis_ref[...].astype(jnp.float32))
     inner = work[:, K : K + 1] * (1.0 / math.sqrt(TOTAL))
-    coeff_ref[...] = jnp.sum(jnp.where(at_lane == at_row, inner, 0.0), axis=0, keepdims=True)
+    coeff_ref[...] = jnp.sum(jnp.where(at_lane == at_row, inner, 0.0), axis=0)[:K]
 
 
 def summed(array, axes, count):
@@ -92,8 +95,9 @@
     params = pltpu.CompilerParams(vmem_limit_bytes=VMEM)
     smem = pl.BlockSpec(memory_space=pltpu.SMEM)
     vmem = pl.BlockSpec(memory_space=pltpu.VMEM)
-    ordered = jnp.where(old_id[0] % 2 == 0, old_basis, old_basis[::-1])
-    sideways = ordered.reshape(2, BLK, K).transpose(2, 0, 1).reshape(K, PAIR)
+    first, second = (old_basis[i].reshape(BLK, K).T for i in (0, 1))
+    kept = old_id[0] % 2 == 0
+    sideways = jnp.concatenate([jnp.where(kept, first, second), jnp.where(kept, second, first)], axis=1)
     placed = lax.ppermute(sideways, COL, [(i, (i + 1) % N_COL) for i in range(N_COL)])
     copies = jnp.broadcast_to(placed[None], (N_ROW, K, PAIR))
     col_basis = lax.all_to_all(copies, ROW, 0, 0, tiled=True)
@@ -105,9 +109,9 @@
         scratch_shapes=[pltpu.VMEM((2 * N_ROW, K, BLK), jnp.bfloat16)],
         compiler_params=params,
     )(block_row.reshape(NNZ), block_col.reshape(NNZ), tile_count.reshape(1), tangent.reshape(NNZ, BLK, BLK), col_basis)
-    over_x = lax.all_to_all(partial, "x", 0, 0, tiled=True)
-    over_x = jnp.sum(over_x.reshape(N_X, N_Z, K, PAIR), axis=0)
-    over_z = lax.all_to_all(over_x, "z", 0, 0, tiled=True)
+    near = lax.all_to_all(partial, NEAR, 0, 0, tiled=True)
+    near = jnp.sum(near.reshape(N_NEAR, N_Z_HI, K, PAIR), axis=0)
+    far = lax.all_to_all(near, "z_hi", 0, 0, tiled=True)
     product, gram = pl.pallas_call(
         gram_kernel,
         out_shape=(
@@ -117,26 +121,26 @@
         in_specs=[vmem, vmem],
         out_specs=(vmem, vmem),
         compiler_params=params,
-    )(over_z, residual.reshape(1, PAIR))
-    gram = summed(gram, "x", N_X)
+    )(far, residual.reshape(1, PAIR))
+    gram = summed(gram, NEAR, N_NEAR)
     gram = summed(gram, ROW, N_ROW)
-    gram = summed(gram, "z", N_Z)
+    gram = summed(gram, "z_hi", N_Z_HI)
     out_c, out_u, coefficients = pl.pallas_call(
         finish_kernel,
         out_shape=(
             jax.ShapeDtypeStruct((PAIR, K), jnp.bfloat16),
             jax.ShapeDtypeStruct((PAIR, K), jnp.bfloat16),
-            jax.ShapeDtypeStruct((1, PAIR), jnp.float32),
+            jax.ShapeDtypeStruct((K,), jnp.float32),
         ),
         in_specs=[vmem, vmem, vmem],
         out_specs=(vmem, vmem, vmem),
         compiler_params=params,
     )(gram, product, placed)
-    return (out_c.reshape(2, BLK * K), out_u.reshape(2, BLK * K), coefficients[0, :K])
+    return (out_c.reshape(2, BLK * K), out_u.reshape(2, BLK * K), coefficients)
 
 
 def solution(mesh):
-    split = Mesh(mesh.devices.reshape(N_Y, N_CORE, N_Z, N_X), ("y", "core", "z", "x"))
+    split = Mesh(mesh.devices.reshape(N_Y, N_CORE, N_Z_HI, N_Z_LO, N_X), ROW + COL)
     return jax.shard_map(
         per_device,
         mesh=split,

time: 159 us -> 143 us (0.90); the launches traced: 156 us -> 142 us
  local copies, waits for them, and re-layouts: 13.1 us -> 4.59 us
  blocking collectives: 93.8 us -> 87.2 us
    rev x1 -> x0, local copies, waits for them, and re-layouts: 8.16 us -> none  [per_device(): ordered = jnp.where(old_id[0] % 2 == 0, old_basis, old_basis[::-1])]
    all_to_all x2, blocking collectives: 47.3 us -> 43.6 us  [the longest x1 23.7 us: per_device(): near = lax.all_to_all(partial, NEAR, 0, 0, tiled=True)]
    all_to_all x3, blocking collectives: 46.5 us -> 43.6 us  [summed(): return jnp.sum(lax.all_to_all(copies, axes, 0, 0, tiled=True), axis=0)]
where the time goes in v2:
time: 143 us; the launch traced here: 142 us
  blocking collectives  87.2 us (61%)
  waiting for transfers between devices  25.7 us (18%)
  starting transfers between devices  12.6 us (9%)
  Pallas kernels  7.94 us (6%)
  local copies, waits for them, and re-layouts  4.59 us (3%)
  between operations  3.35 us (2%)
    all_to_all x3, blocking collectives, summed(): return jnp.sum(lax.all_to_all(copies, axes, 0, 0, tiled=True), axis=0)  43.6 us
    all_to_all x1, blocking collectives, per_device(): near = lax.all_to_all(partial, NEAR, 0, 0, tiled=True)  23.7 us
    all_to_all x1, blocking collectives, per_device(): far = lax.all_to_all(near, 'z_hi', 0, 0, tiled=True)  19.9 us
    ppermute x1, waiting for transfers between devices, per_device(): lax.ppermute(sideways, COL, [(i, (i + 1) % N_COL) for i in range(N_COL)])  18.1 us
    all_to_all x1, starting transfers between devices, per_device(): col_basis = lax.all_to_all(copies, ROW, 0, 0, tiled=True)  8.66 us
    all_to_all x1, waiting for transfers between devices, per_device(): col_basis = lax.all_to_all(copies, ROW, 0, 0, tiled=True)  7.61 us
    pallas_call x1, Pallas kernels, per_device(): pl.pallas_call(finish_kernel, out_shape=(jax.ShapeDtypeStruct((PAIR, K),...  4.55 us
    ppermute x1, starting transfers between devices, per_device(): lax.ppermute(sideways, COL, [(i, (i + 1) % N_COL) for i in range(N_COL)])  3.95 us
  transfers between devices with their start and end apart: 2, of which 2 were waited for; matrix products, arithmetic and copies ran while one was open for 1% of the time, Pallas kernels for 0%

profile of v2, /device:TPU:1, one launch (start us, length us, event | category | flops | bytes accessed | tf_op | source)
XLA Modules:
  0.0 142.5 jit_solution(7937759021426932923)
XLA Ops:
  0.6 0.0 copy-start.2
  0.6 0.0 copy-start.1
  2.6 0.9 fusion
  3.5 0.1 select_n.34
  3.6 0.1 copy.12
  3.7 0.1 select_n.37
  3.8 0.1 copy.13
  3.9 0.1 pad_maximum_fusion
  3.9 4.0 %collective-permute-start = (bf16[48,128]{1,0:T(8,128)(2,1)S(1)}, bf16[48,128]{1,0:T(8,128)(2,1)S(1)}, u32[]{:S(2)}, u32[]{:S(2)}) collective-permute-start(bf16[48,128]{1,0:T(8,128)(2,1)S(1)} %pad_maximum_fusion), channel_id=1, source_target_pairs={{0,1},{1,2},{2,3},{3,4},{4,5},{5,6},{6,7},{7,8},{8,9},{9,10},{10,1... | collective-permute-start | bytes 36872 | tf_op jit(solution)/shard_map/ppermute | solution.py:101
  7.9 18.1 %collective-permute-done.basis_ref = bf16[48,128]{1,0:T(8,128)(2,1)S(1)} collective-permute-done((bf16[48,128]{1,0:T(8,128)(2,1)S(1)}, bf16[48,128]{1,0:T(8,128)(2,1)S(1)}, u32[]{:S(2)}, u32[]{:S(2)}) %collective-permute-start) | collective-permute-done | bytes 12320 | tf_op jit(solution)/shard_map/ppermute | solution.py:101
  26.0 0.7 broadcast_in_dim.8
  26.7 8.7 %all-to-all-start = ((bf16[16,48,128]{2,1,0:T(8,128)(2,1)}), bf16[16,48,128]{2,1,0:T(8,128)(2,1)S(1)}, u32[]{:S(2)}, u32[]{:S(2)}) async-start(bf16[16,48,128]{2,1,0:T(8,128)(2,1)} %broadcast_in_dim.8), calls=%async_computation | async-start | bytes 393216 | tf_op jit(solution)/shard_map/all_to_all | solution.py:103
  36.0 2.1 %reshape.41.tangent_ref = bf16[64,64,64]{2,1,0:T(8,128)(2,1)S(1)} reshape(bf16[1,1,64,4096]{3,2,1,0:T(8,128)(2,1)} %param.7) | data formatting | bytes 1048576 | tf_op jit(solution)/shard_map/reshape | solution.py:111
  38.1 7.6 %all-to-all-done.basis_ref = bf16[16,48,128]{2,1,0:T(8,128)(2,1)S(1)} async-done(((bf16[16,48,128]{2,1,0:T(8,128)(2,1)}), bf16[16,48,128]{2,1,0:T(8,128)(2,1)S(1)}, u32[]{:S(2)}, u32[]{:S(2)}) %all-to-all-start) | async-done | bytes 196640 | tf_op jit(solution)/shard_map/all_to_all | solution.py:103
  45.7 0.0 copy-done.2
  45.7 0.0 copy-done.1
  45.7 3.2 %shard_map.94 = f32[64,48,128]{2,1,0:T(8,128)S(1)} custom-call(s32[64]{0:T(128)S(1)} %bitcast.13, s32[64]{0:T(128)S(1)} %bitcast.14, s32[1]{0:T(128)} %bitcast.11.count_ref, bf16[64,64,64]{2,1,0:T(8,128)(2,1)S(1)} %reshape.41.tangent_ref, bf16[16,48,128]{2,1,0:T(8,128)(2,1)S(1)} %all-to-all-done.basis_ref), custom_call_target="tpu_custom_call" | custom-call | tf_op jit(solution)/shard_map/pallas_call | solution.py:104
  48.8 23.7 %all_to_all.30 = f32[64,48,128]{2,1,0:T(8,128)S(1)} all-to-all(f32[64,48,128]{2,1,0:T(8,128)S(1)} %shard_map.94), channel_id=1, replica_groups=mesh['y'=8,'core'=2,'z_hi'=8,'z_lo'=2,'x'=4] {'z_lo','x'}, dimensions={0} | all-to-all | bytes 3145728 | tf_op jit(solution)/shard_map/all_to_all | solution.py:112
  72.5 0.0 copy-start
  72.5 0.1 reduce_sum.36
  72.6 19.9 %all_to_all.31.parts_ref = f32[8,48,128]{2,1,0:T(8,128)S(1)} all-to-all(f32[8,48,128]{2,1,0:T(8,128)S(1)} %reduce_sum.36), channel_id=1, replica_groups=mesh['y'=8,'core'=2,'z_hi'=8,'z_lo'=2,'x'=4] {'z_hi'}, dimensions={0} | all-to-all | bytes 393216 | tf_op jit(solution)/shard_map/all_to_all | solution.py:114
  92.5 0.0 copy-done
  92.5 0.2 shard_map.95
  92.8 9.3 %all_to_all.32 = f32[8,24,128]{2,1,0:T(8,128)S(1)} all-to-all(f32[8,24,128]{2,1,0:T(8,128)S(1)} %broadcast_in_dim.9), channel_id=1, replica_groups=mesh['y'=8,'core'=2,'z_hi'=8,'z_lo'=2,'x'=4] {'z_lo','x'}, dimensions={0} | all-to-all | bytes 196608 | tf_op jit(solution)/shard_map/all_to_all | solution.py:91
  102.1 17.4 %all_to_all.33 = f32[16,24,128]{2,1,0:T(8,128)S(1)} all-to-all(f32[16,24,128]{2,1,0:T(8,128)S(1)} %broadcast_in_dim.10), channel_id=1, replica_groups=mesh['y'=8,'core'=2,'z_hi'=8,'z_lo'=2,'x'=4] {'y','core'}, dimensions={0} | all-to-all | bytes 393216 | tf_op jit(solution)/shard_map/all_to_all | solution.py:91
  119.6 16.9 %all_to_all.34 = f32[8,24,128]{2,1,0:T(8,128)S(1)} all-to-all(f32[8,24,128]{2,1,0:T(8,128)S(1)} %broadcast_in_dim.11), channel_id=1, replica_groups=mesh['y'=8,'core'=2,'z_hi'=8,'z_lo'=2,'x'=4] {'z_hi'}, dimensions={0} | all-to-all | bytes 196608 | tf_op jit(solution)/shard_map/all_to_all | solution.py:91
  136.5 4.6 %shard_map.96 = (bf16[128,48]{1,0:T(8,128)(2,1)S(1)}, bf16[128,48]{1,0:T(8,128)(2,1)S(1)}, f32[48]{0:T(128)}) custom-call(f32[24,128]{1,0:T(8,128)S(1)} %reduce_sum.39.gram_ref, f32[48,128]{1,0:T(8,128)S(1)} %get-tuple-element.9.product_ref, bf16[48,128]{1,0:T(8,128)(2,1)S(1)} %collective-permute-done.basis_ref), custom_call_target="tpu_custom_call" | custom-call | tf_op jit(solution)/shard_map/pallas_call | solution.py:128
  141.1 0.7 reshape.44
  141.8 0.7 reshape.45
  (6 shorter events, 0.1 us)
Async XLA Ops:
  0.6 45.0 %copy-start.2 = (s32[1,1,64]{2,1,0:T(1,128)S(1)}, s32[1,1,64]{2,1,0:T(1,128)}, u32[]{:S(2)}) copy-start(s32[1,1,64]{2,1,0:T(1,128)} %param.9) | copy-start | bytes 772
  0.6 45.0 %copy-start.1 = (s32[1,1,64]{2,1,0:T(1,128)S(1)}, s32[1,1,64]{2,1,0:T(1,128)}, u32[]{:S(2)}) copy-start(s32[1,1,64]{2,1,0:T(1,128)} %param.8) | copy-start | bytes 772
  3.9 22.0 %collective-permute-start = (bf16[48,128]{1,0:T(8,128)(2,1)S(1)}, bf16[48,128]{1,0:T(8,128)(2,1)S(1)}, u32[]{:S(2)}, u32[]{:S(2)}) collective-permute-start(bf16[48,128]{1,0:T(8,128)(2,1)S(1)} %pad_maximum_fusion), channel_id=1, source_target_pairs={{0,1},{1,2},{2,3},{3,4},{4,5},{5,6},{6,7},{7,8},{8,9},{9,10},{10,1... | collective-permute-start | bytes 36872 | tf_op jit(solution)/shard_map/ppermute | solution.py:101
  26.7 19.0 %all-to-all-start = ((bf16[16,48,128]{2,1,0:T(8,128)(2,1)}), bf16[16,48,128]{2,1,0:T(8,128)(2,1)S(1)}, u32[]{:S(2)}, u32[]{:S(2)}) async-start(bf16[16,48,128]{2,1,0:T(8,128)(2,1)} %broadcast_in_dim.8), calls=%async_computation | async-start | bytes 393216 | tf_op jit(solution)/shard_map/all_to_all | solution.py:103
  72.5 20.0 %copy-start = (f32[128]{0:T(128)S(1)}, f32[128]{0:T(128)}, u32[]{:S(2)}) copy-start(f32[128]{0:T(128)} %param.13) | copy-start | bytes 1540

commit v3 on v2

--- a/solution.py
+++ b/solution.py
@@ -25,11 +25,94 @@
 VMEM = 48 * 1024 * 1024
 
 
-def product_kernel(row_ref, col_ref, count_ref, tangent_ref, basis_ref, out_ref, half_ref):
+HALF = BLK // 4
+SHIFT = K
+INNER = 2 * K
+WORDS = 2 * HALF
+STEPS = (64, 32, 16, 8, 4, 2, 1)
+LOWEST = 100
+MAGIC = 12582912.0
+
+
+def encode(sums_ref, count, out_ref):
+    def look(i, peak):
+        return jnp.maximum(peak, jnp.abs(sums_ref[i]))
+
+    peak = lax.fori_loop(0, count, look, jnp.zeros((K, PAIR), jnp.float32), unroll=8)
+    peak = jnp.broadcast_to(jnp.max(peak, axis=1, keepdims=True), (K, PAIR))
+    factor = jnp.full((K, PAIR), 2.0**19, jnp.float32)
+    power = jnp.zeros((K, PAIR), jnp.int32)
+    for step in STEPS:
+        big = peak >= 2.0**step
+        peak = jnp.where(big, peak * 2.0**-step, peak)
+        factor = jnp.where(big, factor * 2.0**-step, factor)
+        power = jnp.where(big, power + step, power)
+    for step in STEPS:
+        small = (peak < 2.0 ** (1 - step)) & (power - step >= -LOWEST)
+        peak = jnp.where(small, peak * 2.0**step, peak)
+        factor = jnp.where(small, factor * 2.0**step, factor)
+        power = jnp.where(small, power - step, power)
+    power = power + LOWEST
+    lane = lax.broadcasted_iota(jnp.int32, (HALF, PAIR), 1)
+    shown = jnp.where(lane < 8, power[:HALF], jnp.where(lane < 16, power[HALF:WORDS], power[WORDS:]))
+    flags = ((shown >> (lane & 7)) & 1) << 10
+
+    def put(i, carry):
+        code = ((sums_ref[i] * factor + MAGIC) - MAGIC).astype(jnp.int32)
+        code = jnp.minimum(code, (1 << 20) - 1)
+        third = code[WORDS:]
+        out_ref[i, :HALF] = (code[:HALF] << 11) | ((third >> 10) & 0x7FF)
+        out_ref[i, HALF:] = (code[HALF:WORDS] << 11) | (third & 0x3FF) | flags
+        return carry
+
+    lax.fori_loop(0, count, put, 0, unroll=8)
+
+
+def unit_of(second):
+    lane = lax.broadcasted_iota(jnp.int32, (HALF, PAIR), 1)
+    bits = (((second >> 10) & 1) << (lane & 7)).astype(jnp.float32)
+    power = jnp.concatenate(
+        [
+            jnp.sum(jnp.where((lane >= 8 * i) & (lane < 8 * i + 8), bits, 0.0), axis=1, keepdims=True)
+            for i in range(3)
+        ],
+        axis=0,
+    )
+    power = jnp.broadcast_to(power, (K, PAIR)).astype(jnp.int32)
+    unit = jnp.full((K, PAIR), 2.0 ** (-LOWEST - 19), jnp.float32)
+    for i in range(8):
+        steps = (2.0 ** (1 << i),) if i < 7 else (2.0**64, 2.0**64)
+        for step in steps:
+            unit = jnp.where(((power >> i) & 1) == 1, unit * step, unit)
+    return unit
+
+
+def decode(words):
+    first, second = words[:HALF], words[HALF:]
+    third = ((first << 21) >> 11) | (second & 0x3FF)
+    return jnp.concatenate([first >> 11, second >> 11, third], axis=0).astype(jnp.float32)
+
+
+def near_kernel(near_ref, out_ref, unit_ref, sums_ref):
+    for source in range(N_NEAR):
+        unit_ref[source] = unit_of(near_ref[source, 0, HALF:])
+
+    def add(i, carry):
+        total = decode(near_ref[0, i]) * unit_ref[0]
+        for source in range(1, N_NEAR):
+            total += decode(near_ref[source, i]) * unit_ref[source]
+        sums_ref[i] = total
+        return carry
+
+    lax.fori_loop(0, N_Z_HI, add, 0)
+    encode(sums_ref, N_Z_HI, out_ref)
+
+
+def product_kernel(row_ref, col_ref, count_ref, tangent_ref, basis_ref, out_ref, half_ref, sums_ref):
     for q in range(N_ROW):
         half_ref[2 * q] = basis_ref[q, :, :BLK]
         half_ref[2 * q + 1] = basis_ref[q, :, BLK:]
-    out_ref[...] = jnp.zeros_like(out_ref)
+    sums_ref[...] = jnp.zeros_like(sums_ref)
     count = count_ref[0]
 
     def add_block(n, carry):
@@ -40,49 +123,62 @@
         block = tangent_ref[n]
         none = jnp.zeros_like(block)
         sides = jnp.concatenate([jnp.where(side == 0, block, none), jnp.where(side == 1, block, none)], axis=0)
-        out_ref[place] += lax.dot_general(
+        sums_ref[place] += lax.dot_general(
             half_ref[col_ref[n]], sides, (((1,), (1,)), ((), ())), preferred_element_type=jnp.float32
         )
         return carry
 
     lax.fori_loop(0, NNZ, add_block, 0, unroll=8)
-
-
-def gram_kernel(parts_ref, residual_ref, product_ref, gram_ref):
-    product = jnp.sum(parts_ref[...], axis=0)
+    encode(sums_ref, N_COL, out_ref)
+
+
+def gram_kernel(far_ref, residual_ref, product_ref, gram_ref):
+    product = decode(far_ref[0]) * unit_of(far_ref[0, HALF:])
+    for source in range(1, N_Z_HI):
+        product += decode(far_ref[source]) * unit_of(far_ref[source, HALF:])
     product_ref[...] = product
-    first = lax.broadcasted_iota(jnp.int32, (16, PAIR), 0) == 0
-    extra = jnp.where(first, jnp.broadcast_to(residual_ref[...], (16, PAIR)), 0.0)
+    at_row = lax.broadcasted_iota(jnp.int32, (PAIR - K, PAIR), 0)
+    extra = jnp.where((at_row == 1) | (at_row == K), residual_ref[...], 0.0)
     both = jnp.concatenate([product, extra], axis=0)
     gram = lax.dot_general(product, both, (((1,), (1,)), ((), ())), precision=HIGHEST)
-    gram_ref[...] = jnp.concatenate([gram[: K // 2], gram[K // 2 :]], axis=1)
+    lane = lax.broadcasted_iota(jnp.int32, (HALF, PAIR), 1)
+    top, middle, bottom = gram[:HALF], gram[HALF:WORDS], gram[WORDS:]
+    gram_ref[...] = jnp.where(
+        (lane < K) | (lane == 96),
+        bottom,
+        jnp.where((lane < 80) | (lane == 97), pltpu.roll(middle, 48, 1), pltpu.roll(top, 112, 1)),
+    )
 
 
 def finish_kernel(gram_ref, product_ref, basis_ref, out_c_ref, out_u_ref, coeff_ref):
     packed = gram_ref[...]
-    upper = jnp.concatenate([packed[:, :BLK], packed[:, BLK:]], axis=0)
-    work = jnp.concatenate([upper, jnp.zeros_like(upper)], axis=1)
+    top = pltpu.roll(packed, 16, 1)
+    blocks = jnp.concatenate([top, pltpu.roll(packed, 80, 1), packed], axis=0)
+    inner = jnp.concatenate([top, pltpu.roll(packed, 127, 1), packed], axis=0)
     at_row = lax.broadcasted_iota(jnp.int32, (K, PAIR), 0)
     at_lane = lax.broadcasted_iota(jnp.int32, (K, PAIR), 1)
-    work = jnp.where(at_lane < K, work * (1.0 / TOTAL), work)
-    work = jnp.where(at_lane == at_row + BLK, 1.0, work)
+    blocks = blocks * (1.0 / TOTAL)
+    below = jnp.concatenate([jnp.where(at_lane < at_row, blocks, 0.0), jnp.zeros((PAIR - K, PAIR), jnp.float32)], axis=0)
+    work = jnp.where(at_lane <= at_row, blocks, below.T[:K])
+    work = jnp.where(at_lane == INNER, inner, work)
+    work = jnp.where(at_lane == at_row + SHIFT, 1.0, work)
     for k in range(K - 1):
         pivot_row = work[k : k + 1, :]
         factor = work[:, k : k + 1] / pivot_row[:, k : k + 1]
         work = work - jnp.where(at_row > k, factor * pivot_row, 0.0)
     pivots = jnp.sum(jnp.where(at_lane == at_row, work, 0.0), axis=1, keepdims=True)
     work = work / jnp.sqrt(pivots)
-    inverse = jnp.where(at_lane >= BLK, work, 0.0)
+    inverse = jnp.where((at_lane >= SHIFT) & (at_lane < INNER), work, 0.0)
 
     def transformed(columns):
         tall = jnp.concatenate(
-            [jnp.zeros((BLK, PAIR), jnp.float32), columns, jnp.zeros((BLK - K, PAIR), jnp.float32)], axis=0
+            [jnp.zeros((SHIFT, PAIR), jnp.float32), columns, jnp.zeros((PAIR - INNER, PAIR), jnp.float32)], axis=0
         )
         return jnp.dot(inverse, tall, precision=HIGHEST).T.astype(jnp.bfloat16)
 
     out_c_ref[...] = transformed(product_ref[...])
     out_u_ref[...] = transformed(basis_ref[...].astype(jnp.float32))
-    inner = work[:, K : K + 1] * (1.0 / math.sqrt(TOTAL))
+    inner = work[:, INNER : INNER + 1] * (1.0 / math.sqrt(TOTAL))
     coeff_ref[...] = jnp.sum(jnp.where(at_lane == at_row, inner, 0.0), axis=0)[:K]
 
 
@@ -99,24 +195,32 @@
     kept = old_id[0] % 2 == 0
     sideways = jnp.concatenate([jnp.where(kept, first, second), jnp.where(kept, second, first)], axis=1)
     placed = lax.ppermute(sideways, COL, [(i, (i + 1) % N_COL) for i in range(N_COL)])
-    copies = jnp.broadcast_to(placed[None], (N_ROW, K, PAIR))
+    blocks, sent = lax.optimization_barrier((tangent.reshape(NNZ, BLK, BLK), placed))
+    copies = jnp.broadcast_to(sent[None], (N_ROW, K, PAIR))
     col_basis = lax.all_to_all(copies, ROW, 0, 0, tiled=True)
     partial = pl.pallas_call(
         product_kernel,
-        out_shape=jax.ShapeDtypeStruct((N_COL, K, PAIR), jnp.float32),
+        out_shape=jax.ShapeDtypeStruct((N_COL, WORDS, PAIR), jnp.int32),
         in_specs=[smem, smem, smem, vmem, vmem],
         out_specs=vmem,
-        scratch_shapes=[pltpu.VMEM((2 * N_ROW, K, BLK), jnp.bfloat16)],
-        compiler_params=params,
-    )(block_row.reshape(NNZ), block_col.reshape(NNZ), tile_count.reshape(1), tangent.reshape(NNZ, BLK, BLK), col_basis)
+        scratch_shapes=[pltpu.VMEM((2 * N_ROW, K, BLK), jnp.bfloat16), pltpu.VMEM((N_COL, K, PAIR), jnp.float32)],
+        compiler_params=params,
+    )(block_row.reshape(NNZ), block_col.reshape(NNZ), tile_count.reshape(1), blocks, col_basis)
     near = lax.all_to_all(partial, NEAR, 0, 0, tiled=True)
-    near = jnp.sum(near.reshape(N_NEAR, N_Z_HI, K, PAIR), axis=0)
+    near = pl.pallas_call(
+        near_kernel,
+        out_shape=jax.ShapeDtypeStruct((N_Z_HI, WORDS, PAIR), jnp.int32),
+        in_specs=[vmem],
+        out_specs=vmem,
+        scratch_shapes=[pltpu.VMEM((N_NEAR, K, PAIR), jnp.float32), pltpu.VMEM((N_Z_HI, K, PAIR), jnp.float32)],
+        compiler_params=params,
+    )(near.reshape(N_NEAR, N_Z_HI, WORDS, PAIR))
     far = lax.all_to_all(near, "z_hi", 0, 0, tiled=True)
     product, gram = pl.pallas_call(
         gram_kernel,
         out_shape=(
             jax.ShapeDtypeStruct((K, PAIR), jnp.float32),
-            jax.ShapeDtypeStruct((K // 2, PAIR), jnp.float32),
+            jax.ShapeDtypeStruct((HALF, PAIR), jnp.float32),
         ),
         in_specs=[vmem, vmem],
         out_specs=(vmem, vmem),

time: 143 us -> 133 us (0.930)
  blocking collectives: 87.2 us -> 75.8 us
  Pallas kernels: 7.94 us -> 10.4 us
  local copies, waits for them, and re-layouts: 4.59 us -> 6.53 us
  between operations: 3.35 us -> 1.52 us
    all_to_all x1, blocking collectives: 23.7 us -> 18 us  [per_device(): near = lax.all_to_all(partial, NEAR, 0, 0, tiled=True)]
    all_to_all x3, blocking collectives: 43.6 us -> 39.5 us  [summed(): return jnp.sum(lax.all_to_all(copies, axes, 0, 0, tiled=True), axis=0)]
    all_to_all x1, waiting for transfers between devices: 7.61 us -> 9.67 us  [per_device(): col_basis = lax.all_to_all(copies, ROW, 0, 0, tiled=True)]
    ppermute x1, waiting for transfers between devices: 18.1 us -> 16 us  [per_device(): lax.ppermute(sideways, COL, [(i, (i + 1) % N_COL) for i in range(N_COL)])]
    unnamed x6 -> x10, local copies, waits for them, and re-layouts: 0.01 us -> 1.97 us
    pallas_call x1 -> x2, Pallas kernels: 3.16 us -> 4.98 us  [the longest x1 4.01 us: per_device(): pl.pallas_call(product_kernel, out_shape=jax.ShapeDtypeStruct((N_COL, WOR...]
    all_to_all x1, blocking collectives: 19.9 us -> 18.3 us  [per_device(): far = lax.all_to_all(near, 'z_hi', 0, 0, tiled=True)]
  transfers between devices with their start and end apart: 2 -> 2, of which waited for: 2 -> 2; matrix products, arithmetic and copies ran while one was open for 1% -> 2% of each run, Pallas kernels for 0% -> 0%
where the time goes in v3:
time: 133 us
  blocking collectives  75.8 us (57%)
  waiting for transfers between devices  25.7 us (19%)
  starting transfers between devices  12.6 us (9%)
  Pallas kernels  10.4 us (8%)
  local copies, waits for them, and re-layouts  6.53 us (5%)
  between operations  1.52 us (1%)
    all_to_all x3, blocking collectives, summed(): return jnp.sum(lax.all_to_all(copies, axes, 0, 0, tiled=True), axis=0)  39.5 us
    all_to_all x1, blocking collectives, per_device(): far = lax.all_to_all(near, 'z_hi', 0, 0, tiled=True)  18.3 us
    all_to_all x1, blocking collectives, per_device(): near = lax.all_to_all(partial, NEAR, 0, 0, tiled=True)  18 us
    ppermute x1, waiting for transfers between devices, per_device(): lax.ppermute(sideways, COL, [(i, (i + 1) % N_COL) for i in range(N_COL)])  16 us
    all_to_all x1, waiting for transfers between devices, per_device(): col_basis = lax.all_to_all(copies, ROW, 0, 0, tiled=True)  9.67 us
    all_to_all x1, starting transfers between devices, per_device(): col_basis = lax.all_to_all(copies, ROW, 0, 0, tiled=True)  8.66 us
    pallas_call x1, Pallas kernels, per_device(): pl.pallas_call(finish_kernel, out_shape=(jax.ShapeDtypeStruct((PAIR, K),...  4.71 us
    pallas_call x1, Pallas kernels, per_device(): pl.pallas_call(product_kernel, out_shape=jax.ShapeDtypeStruct((N_COL, WOR...  4.01 us
  transfers between devices with their start and end apart: 2, of which 2 were waited for; matrix products, arithmetic and copies ran while one was open for 2% of the time, Pallas kernels for 0%

profile of v3, /device:TPU:1, one launch (start us, length us, event | category | flops | bytes accessed | tf_op | source)
XLA Modules:
  0.0 132.7 jit_solution(12297877968371430369)
XLA Ops:
  0.6 0.0 copy-start.4
  0.6 0.0 copy-start.3
  0.7 0.6 copy-done.4
  1.4 0.0 copy-done.3
  1.4 0.1 fusion
  1.5 0.1 select_n.34
  1.6 0.1 copy.12
  1.7 0.1 select_n.37
  1.8 0.1 copy.13
  1.9 0.1 pad_maximum_fusion
  2.0 4.0 %collective-permute-start = (bf16[48,128]{1,0:T(8,128)(2,1)S(1)}, bf16[48,128]{1,0:T(8,128)(2,1)S(1)}, u32[]{:S(2)}, u32[]{:S(2)}) collective-permute-start(bf16[48,128]{1,0:T(8,128)(2,1)S(1)} %pad_maximum_fusion), channel_id=1, source_target_pairs={{0,1},{1,2},{2,3},{3,4},{4,5},{5,6},{6,7},{7,8},{8,9},{9,10},{10,1... | collective-permute-start | bytes 36872 | tf_op jit(solution)/shard_map/ppermute | solution.py:197
  5.9 2.1 %reshape.41.tangent_ref = bf16[64,64,64]{2,1,0:T(8,128)(2,1)S(1)} reshape(bf16[1,1,64,4096]{3,2,1,0:T(8,128)(2,1)} %param.7) | data formatting | bytes 1048576 | tf_op jit(solution)/shard_map/reshape | solution.py:198
  8.0 16.0 %collective-permute-done.basis_ref = bf16[48,128]{1,0:T(8,128)(2,1)S(1)} collective-permute-done((bf16[48,128]{1,0:T(8,128)(2,1)S(1)}, bf16[48,128]{1,0:T(8,128)(2,1)S(1)}, u32[]{:S(2)}, u32[]{:S(2)}) %collective-permute-start) | collective-permute-done | bytes 12320 | tf_op jit(solution)/shard_map/ppermute | solution.py:197
  24.0 0.7 broadcast_in_dim.8
  24.7 8.7 %all-to-all-start = ((bf16[16,48,128]{2,1,0:T(8,128)(2,1)}), bf16[16,48,128]{2,1,0:T(8,128)(2,1)S(1)}, u32[]{:S(2)}, u32[]{:S(2)}) async-start(bf16[16,48,128]{2,1,0:T(8,128)(2,1)} %broadcast_in_dim.8), calls=%async_computation | async-start | bytes 393216 | tf_op jit(solution)/shard_map/all_to_all | solution.py:200
  34.0 9.7 %all-to-all-done.basis_ref = bf16[16,48,128]{2,1,0:T(8,128)(2,1)S(1)} async-done(((bf16[16,48,128]{2,1,0:T(8,128)(2,1)}), bf16[16,48,128]{2,1,0:T(8,128)(2,1)S(1)}, u32[]{:S(2)}, u32[]{:S(2)}) %all-to-all-start) | async-done | bytes 196640 | tf_op jit(solution)/shard_map/all_to_all | solution.py:200
  43.7 0.0 copy-start
  43.7 0.0 copy-start.1
  43.7 0.7 copy-done
  44.3 0.0 copy-done.1
  44.4 4.0 %shard_map.94 = s32[64,32,128]{2,1,0:T(8,128)S(1)} custom-call(s32[64]{0:T(128)S(1)} %bitcast.13, s32[64]{0:T(128)S(1)} %bitcast.14, s32[1]{0:T(128)} %bitcast.11.count_ref, bf16[64,64,64]{2,1,0:T(8,128)(2,1)S(1)} %reshape.41.tangent_ref, bf16[16,48,128]{2,1,0:T(8,128)(2,1)S(1)} %all-to-all-done.basis_ref), custom_call_target="tpu_custom_call" | custom-call | tf_op jit(solution)/shard_map/pallas_call | solution.py:201
  48.4 18.0 %all_to_all.30 = s32[64,32,128]{2,1,0:T(8,128)S(1)} all-to-all(s32[64,32,128]{2,1,0:T(8,128)S(1)} %shard_map.94), channel_id=1, replica_groups=mesh['y'=8,'core'=2,'z_hi'=8,'z_lo'=2,'x'=4] {'z_lo','x'}, dimensions={0} | all-to-all | bytes 2097152 | tf_op jit(solution)/shard_map/all_to_all | solution.py:209
  66.3 1.0 shard_map.95
  67.3 18.3 %all_to_all.31.far_ref = s32[8,32,128]{2,1,0:T(8,128)S(1)} all-to-all(s32[8,32,128]{2,1,0:T(8,128)S(1)} %shard_map.95), channel_id=1, replica_groups=mesh['y'=8,'core'=2,'z_hi'=8,'z_lo'=2,'x'=4] {'z_hi'}, dimensions={0} | all-to-all | bytes 262144 | tf_op jit(solution)/shard_map/all_to_all | solution.py:218
  85.6 0.0 copy-start.2
  85.6 0.7 copy-done.2
  86.3 0.7 shard_map.96
  87.0 8.6 %all_to_all.32 = f32[8,16,128]{2,1,0:T(8,128)S(1)} all-to-all(f32[8,16,128]{2,1,0:T(8,128)S(1)} %broadcast_in_dim.9), channel_id=1, replica_groups=mesh['y'=8,'core'=2,'z_hi'=8,'z_lo'=2,'x'=4] {'z_lo','x'}, dimensions={0} | all-to-all | bytes 131072 | tf_op jit(solution)/shard_map/all_to_all | solution.py:187
  95.6 15.8 %all_to_all.33 = f32[16,16,128]{2,1,0:T(8,128)S(1)} all-to-all(f32[16,16,128]{2,1,0:T(8,128)S(1)} %broadcast_in_dim.10), channel_id=1, replica_groups=mesh['y'=8,'core'=2,'z_hi'=8,'z_lo'=2,'x'=4] {'y','core'}, dimensions={0} | all-to-all | bytes 262144 | tf_op jit(solution)/shard_map/all_to_all | solution.py:187
  111.5 15.1 %all_to_all.34 = f32[8,16,128]{2,1,0:T(8,128)S(1)} all-to-all(f32[8,16,128]{2,1,0:T(8,128)S(1)} %broadcast_in_dim.11), channel_id=1, replica_groups=mesh['y'=8,'core'=2,'z_hi'=8,'z_lo'=2,'x'=4] {'z_hi'}, dimensions={0} | all-to-all | bytes 131072 | tf_op jit(solution)/shard_map/all_to_all | solution.py:187
  126.6 4.7 %shard_map.97 = (bf16[128,48]{1,0:T(8,128)(2,1)S(1)}, bf16[128,48]{1,0:T(8,128)(2,1)S(1)}, f32[48]{0:T(128)}) custom-call(f32[16,128]{1,0:T(8,128)S(1)} %reduce_sum.29.gram_ref, f32[48,128]{1,0:T(8,128)S(1)} %get-tuple-element.13.product_ref, bf16[48,128]{1,0:T(8,128)(2,1)S(1)} %collective-permute-done.basis_ref), custom_call_target="tpu_custom_call" | custom-call | tf_op jit(solution)/shard_map/pallas_call | solution.py:232
  131.3 0.7 reshape.44
  132.0 0.7 reshape.45
  (6 shorter events, 0.1 us)
Async XLA Ops:
  0.6 0.7 copy-start.4
  0.6 0.8 copy-start.3
  2.0 22.0 %collective-permute-start = (bf16[48,128]{1,0:T(8,128)(2,1)S(1)}, bf16[48,128]{1,0:T(8,128)(2,1)S(1)}, u32[]{:S(2)}, u32[]{:S(2)}) collective-permute-start(bf16[48,128]{1,0:T(8,128)(2,1)S(1)} %pad_maximum_fusion), channel_id=1, source_target_pairs={{0,1},{1,2},{2,3},{3,4},{4,5},{5,6},{6,7},{7,8},{8,9},{9,10},{10,1... | collective-permute-start | bytes 36872 | tf_op jit(solution)/shard_map/ppermute | solution.py:197
  24.7 19.0 %all-to-all-start = ((bf16[16,48,128]{2,1,0:T(8,128)(2,1)}), bf16[16,48,128]{2,1,0:T(8,128)(2,1)S(1)}, u32[]{:S(2)}, u32[]{:S(2)}) async-start(bf16[16,48,128]{2,1,0:T(8,128)(2,1)} %broadcast_in_dim.8), calls=%async_computation | async-start | bytes 393216 | tf_op jit(solution)/shard_map/all_to_all | solution.py:200
  43.7 0.7 copy-start
  43.7 0.7 copy-start.1
  85.6 0.7 copy-start.2

commit v4 on v3

--- a/solution.py
+++ b/solution.py
@@ -108,23 +108,21 @@
     encode(sums_ref, N_Z_HI, out_ref)
 
 
-def product_kernel(row_ref, col_ref, count_ref, tangent_ref, basis_ref, out_ref, half_ref, sums_ref):
+def product_kernel(slot_ref, tangent_ref, basis_ref, out_ref, half_ref, sums_ref):
     for q in range(N_ROW):
         half_ref[2 * q] = basis_ref[q, :, :BLK]
         half_ref[2 * q + 1] = basis_ref[q, :, BLK:]
     sums_ref[...] = jnp.zeros_like(sums_ref)
-    count = count_ref[0]
 
     def add_block(n, carry):
-        row = row_ref[n]
-        owner = row >> 1
-        place = (owner & (N_NEAR - 1)) * N_Z_HI + (owner >> 3)
-        side = jnp.where(n < count, row & 1, 2)
+        slot = slot_ref[n]
+        place = slot & (N_COL - 1)
+        side = (slot >> 6) & 3
         block = tangent_ref[n]
         none = jnp.zeros_like(block)
         sides = jnp.concatenate([jnp.where(side == 0, block, none), jnp.where(side == 1, block, none)], axis=0)
         sums_ref[place] += lax.dot_general(
-            half_ref[col_ref[n]], sides, (((1,), (1,)), ((), ())), preferred_element_type=jnp.float32
+            half_ref[slot >> 8], sides, (((1,), (1,)), ((), ())), preferred_element_type=jnp.float32
         )
         return carry
 
@@ -132,14 +130,12 @@
     encode(sums_ref, N_COL, out_ref)
 
 
-def gram_kernel(far_ref, residual_ref, product_ref, gram_ref):
+def gram_kernel(far_ref, extra_ref, product_ref, gram_ref):
     product = decode(far_ref[0]) * unit_of(far_ref[0, HALF:])
     for source in range(1, N_Z_HI):
         product += decode(far_ref[source]) * unit_of(far_ref[source, HALF:])
     product_ref[...] = product
-    at_row = lax.broadcasted_iota(jnp.int32, (PAIR - K, PAIR), 0)
-    extra = jnp.where((at_row == 1) | (at_row == K), residual_ref[...], 0.0)
-    both = jnp.concatenate([product, extra], axis=0)
+    both = jnp.concatenate([product, extra_ref[...]], axis=0)
     gram = lax.dot_general(product, both, (((1,), (1,)), ((), ())), precision=HIGHEST)
     lane = lax.broadcasted_iota(jnp.int32, (HALF, PAIR), 1)
     top, middle, bottom = gram[:HALF], gram[HALF:WORDS], gram[WORDS:]
@@ -195,17 +191,23 @@
     kept = old_id[0] % 2 == 0
     sideways = jnp.concatenate([jnp.where(kept, first, second), jnp.where(kept, second, first)], axis=1)
     placed = lax.ppermute(sideways, COL, [(i, (i + 1) % N_COL) for i in range(N_COL)])
-    blocks, sent = lax.optimization_barrier((tangent.reshape(NNZ, BLK, BLK), placed))
+    rows, cols = block_row.reshape(NNZ), block_col.reshape(NNZ)
+    owner = rows >> 1
+    side = jnp.where(jnp.arange(NNZ) < tile_count.reshape(1), rows & 1, 2)
+    slots = (owner & (N_NEAR - 1)) * N_Z_HI + (owner >> 3) + (side << 6) + (cols << 8)
+    at_row = lax.broadcasted_iota(jnp.int32, (PAIR - K, PAIR), 0)
+    extra = jnp.where((at_row == 1) | (at_row == K), residual.reshape(1, PAIR), 0.0)
+    blocks, slots, extra, sent = lax.optimization_barrier((tangent.reshape(NNZ, BLK, BLK), slots, extra, placed))
     copies = jnp.broadcast_to(sent[None], (N_ROW, K, PAIR))
     col_basis = lax.all_to_all(copies, ROW, 0, 0, tiled=True)
     partial = pl.pallas_call(
         product_kernel,
         out_shape=jax.ShapeDtypeStruct((N_COL, WORDS, PAIR), jnp.int32),
-        in_specs=[smem, smem, smem, vmem, vmem],
+        in_specs=[smem, vmem, vmem],
         out_specs=vmem,
         scratch_shapes=[pltpu.VMEM((2 * N_ROW, K, BLK), jnp.bfloat16), pltpu.VMEM((N_COL, K, PAIR), jnp.float32)],
         compiler_params=params,
-    )(block_row.reshape(NNZ), block_col.reshape(NNZ), tile_count.reshape(1), blocks, col_basis)
+    )(slots, blocks, col_basis)
     near = lax.all_to_all(partial, NEAR, 0, 0, tiled=True)
     near = pl.pallas_call(
         near_kernel,
@@ -225,7 +227,7 @@
         in_specs=[vmem, vmem],
         out_specs=(vmem, vmem),
         compiler_params=params,
-    )(far, residual.reshape(1, PAIR))
+    )(far, extra)
     gram = summed(gram, NEAR, N_NEAR)
     gram = summed(gram, ROW, N_ROW)
     gram = summed(gram, "z_hi", N_Z_HI)

time: 133 us -> 131 us (0.985)
  blocking collectives: 75.8 us -> 94.3 us
  waiting for transfers between devices: 25.7 us -> 14.6 us
  starting transfers between devices: 12.6 us -> 3.95 us
  local copies, waits for them, and re-layouts: 6.53 us -> 5.19 us
    all_to_all x0 -> x1, blocking collectives: none -> 18.8 us  [per_device(): col_basis = lax.all_to_all(copies, ROW, 0, 0, tiled=True)]
    all_to_all x1 -> x0, waiting for transfers between devices: 9.67 us -> none  [per_device(): col_basis = lax.all_to_all(copies, ROW, 0, 0, tiled=True)]
    all_to_all x1 -> x0, starting transfers between devices: 8.66 us -> none  [per_device(): col_basis = lax.all_to_all(copies, ROW, 0, 0, tiled=True)]
    ppermute x1, waiting for transfers between devices: 16 us -> 14.6 us  [per_device(): lax.ppermute(sideways, COL, [(i, (i + 1) % N_COL) for i in range(N_COL)])]
  transfers between devices with their start and end apart: 2 -> 1, of which waited for: 2 -> 1; matrix products, arithmetic and copies ran while one was open for 2% -> 2% of each run, Pallas kernels for 0% -> 0%
where the time goes in v4:
time: 131 us; the launch traced here: 130 us
  blocking collectives  94.3 us (72%)
  waiting for transfers between devices  14.6 us (11%)
  Pallas kernels  10.4 us (8%)
  local copies, waits for them, and re-layouts  5.19 us (4%)
  starting transfers between devices  3.95 us (3%)
  between operations  1.57 us (1%)
    all_to_all x3, blocking collectives, summed(): return jnp.sum(lax.all_to_all(copies, axes, 0, 0, tiled=True), axis=0)  40.2 us
    all_to_all x1, blocking collectives, per_device(): col_basis = lax.all_to_all(copies, ROW, 0, 0, tiled=True)  18.8 us
    all_to_all x1, blocking collectives, per_device(): near = lax.all_to_all(partial, NEAR, 0, 0, tiled=True)  18 us
    all_to_all x1, blocking collectives, per_device(): far = lax.all_to_all(near, 'z_hi', 0, 0, tiled=True)  17.4 us
    ppermute x1, waiting for transfers between devices, per_device(): lax.ppermute(sideways, COL, [(i, (i + 1) % N_COL) for i in range(N_COL)])  14.6 us
    pallas_call x1, Pallas kernels, per_device(): pl.pallas_call(finish_kernel, out_shape=(jax.ShapeDtypeStruct((PAIR, K),...  4.71 us
    pallas_call x1, Pallas kernels, per_device(): pl.pallas_call(product_kernel, out_shape=jax.ShapeDtypeStruct((N_COL, WOR...  4.02 us
    ppermute x1, starting transfers between devices, per_device(): lax.ppermute(sideways, COL, [(i, (i + 1) % N_COL) for i in range(N_COL)])  3.95 us
  transfers between devices with their start and end apart: 1, of which 1 were waited for; matrix products, arithmetic and copies ran while one was open for 2% of the time, Pallas kernels for 0%

profile of v4, /device:TPU:1, one launch (start us, length us, event | category | flops | bytes accessed | tf_op | source)
XLA Modules:
  0.0 130.3 jit_solution(11480629472521074392)
XLA Ops:
  0.6 0.0 copy-start.2
  0.6 0.0 copy-start
  0.7 0.6 copy-done.2
  1.4 0.0 copy-done
  1.4 0.1 fusion
  1.5 0.1 select_n.44
  1.6 0.1 copy.12
  1.7 0.1 select_n.47
  1.8 0.1 copy.13
  1.9 0.1 pad_maximum_fusion
  2.0 4.0 %collective-permute-start = (bf16[48,128]{1,0:T(8,128)(2,1)S(1)}, bf16[48,128]{1,0:T(8,128)(2,1)S(1)}, u32[]{:S(2)}, u32[]{:S(2)}) collective-permute-start(bf16[48,128]{1,0:T(8,128)(2,1)S(1)} %pad_maximum_fusion), channel_id=1, source_target_pairs={{0,1},{1,2},{2,3},{3,4},{4,5},{5,6},{6,7},{7,8},{8,9},{9,10},{10,1... | collective-permute-start | bytes 36872 | tf_op jit(solution)/shard_map/ppermute | solution.py:193
  5.9 0.0 copy-start.1
  6.6 0.0 copy-done.1
  6.6 0.1 broadcast_select_fusion.2.extra_ref
  6.7 0.0 copy-start.3
  6.7 0.0 copy-start.4
  6.7 0.6 copy-done.3
  7.4 0.0 copy-done.4
  7.4 2.1 %reshape.45.tangent_ref = bf16[64,64,64]{2,1,0:T(8,128)(2,1)S(1)} reshape(bf16[1,1,64,4096]{3,2,1,0:T(8,128)(2,1)} %param.7) | data formatting | bytes 1048576 | tf_op jit(solution)/shard_map/reshape | solution.py:200
  9.4 14.6 %collective-permute-done.basis_ref = bf16[48,128]{1,0:T(8,128)(2,1)S(1)} collective-permute-done((bf16[48,128]{1,0:T(8,128)(2,1)S(1)}, bf16[48,128]{1,0:T(8,128)(2,1)S(1)}, u32[]{:S(2)}, u32[]{:S(2)}) %collective-permute-start) | collective-permute-done | bytes 12320 | tf_op jit(solution)/shard_map/ppermute | solution.py:193
  24.0 18.8 %all_to_all.30.basis_ref = bf16[16,48,128]{2,1,0:T(8,128)(2,1)S(1)} all-to-all(bf16[16,48,128]{2,1,0:T(8,128)(2,1)S(1)} %broadcast_in_dim.43), channel_id=1, replica_groups=mesh['y'=8,'core'=2,'z_hi'=8,'z_lo'=2,'x'=4] {'y','core'}, dimensions={0} | all-to-all | bytes 393216 | tf_op jit(solution)/shard_map/all_to_all | solution.py:202
  42.8 4.0 %shard_map.94 = s32[64,32,128]{2,1,0:T(8,128)S(1)} custom-call(s32[64]{0:T(128)S(1)} %bitcast_add_fusion.slot_ref, bf16[64,64,64]{2,1,0:T(8,128)(2,1)S(1)} %reshape.45.tangent_ref, bf16[16,48,128]{2,1,0:T(8,128)(2,1)S(1)} %all_to_all.30.basis_ref), custom_call_target="tpu_custom_call" | custom-call | tf_op jit(solution)/shard_map/pallas_call | solution.py:203
  46.8 18.0 %all_to_all.31 = s32[64,32,128]{2,1,0:T(8,128)S(1)} all-to-all(s32[64,32,128]{2,1,0:T(8,128)S(1)} %shard_map.94), channel_id=1, replica_groups=mesh['y'=8,'core'=2,'z_hi'=8,'z_lo'=2,'x'=4] {'z_lo','x'}, dimensions={0} | all-to-all | bytes 2097152 | tf_op jit(solution)/shard_map/all_to_all | solution.py:211
  64.8 1.0 shard_map.95
  65.8 17.4 %all_to_all.32.far_ref = s32[8,32,128]{2,1,0:T(8,128)S(1)} all-to-all(s32[8,32,128]{2,1,0:T(8,128)S(1)} %shard_map.95), channel_id=1, replica_groups=mesh['y'=8,'core'=2,'z_hi'=8,'z_lo'=2,'x'=4] {'z_hi'}, dimensions={0} | all-to-all | bytes 262144 | tf_op jit(solution)/shard_map/all_to_all | solution.py:220
  83.1 0.7 shard_map.96
  83.9 9.7 %all_to_all.33 = f32[8,16,128]{2,1,0:T(8,128)S(1)} all-to-all(f32[8,16,128]{2,1,0:T(8,128)S(1)} %broadcast_in_dim.44), channel_id=1, replica_groups=mesh['y'=8,'core'=2,'z_hi'=8,'z_lo'=2,'x'=4] {'z_lo','x'}, dimensions={0} | all-to-all | bytes 131072 | tf_op jit(solution)/shard_map/all_to_all | solution.py:183
  93.7 15.5 %all_to_all.34 = f32[16,16,128]{2,1,0:T(8,128)S(1)} all-to-all(f32[16,16,128]{2,1,0:T(8,128)S(1)} %broadcast_in_dim.45), channel_id=1, replica_groups=mesh['y'=8,'core'=2,'z_hi'=8,'z_lo'=2,'x'=4] {'y','core'}, dimensions={0} | all-to-all | bytes 262144 | tf_op jit(solution)/shard_map/all_to_all | solution.py:183
  109.1 15.0 %all_to_all.35 = f32[8,16,128]{2,1,0:T(8,128)S(1)} all-to-all(f32[8,16,128]{2,1,0:T(8,128)S(1)} %broadcast_in_dim.46), channel_id=1, replica_groups=mesh['y'=8,'core'=2,'z_hi'=8,'z_lo'=2,'x'=4] {'z_hi'}, dimensions={0} | all-to-all | bytes 131072 | tf_op jit(solution)/shard_map/all_to_all | solution.py:183
  124.1 4.7 %shard_map.97 = (bf16[128,48]{1,0:T(8,128)(2,1)S(1)}, bf16[128,48]{1,0:T(8,128)(2,1)S(1)}, f32[48]{0:T(128)}) custom-call(f32[16,128]{1,0:T(8,128)S(1)} %reduce_sum.29.gram_ref, f32[48,128]{1,0:T(8,128)S(1)} %get-tuple-element.17.product_ref, bf16[48,128]{1,0:T(8,128)(2,1)S(1)} %collective-permute-done.basis_ref), custom_call_target="tpu_custom_call" | custom-call | tf_op jit(solution)/shard_map/pallas_call | solution.py:234
  128.9 0.7 reshape.47
  129.6 0.7 reshape.48
  (9 shorter events, 0.1 us)
Async XLA Ops:
  0.6 0.7 copy-start.2
  0.6 0.8 copy-start
  2.0 22.0 %collective-permute-start = (bf16[48,128]{1,0:T(8,128)(2,1)S(1)}, bf16[48,128]{1,0:T(8,128)(2,1)S(1)}, u32[]{:S(2)}, u32[]{:S(2)}) collective-permute-start(bf16[48,128]{1,0:T(8,128)(2,1)S(1)} %pad_maximum_fusion), channel_id=1, source_target_pairs={{0,1},{1,2},{2,3},{3,4},{4,5},{5,6},{6,7},{7,8},{8,9},{9,10},{10,1... | collective-permute-start | bytes 36872 | tf_op jit(solution)/shard_map/ppermute | solution.py:193
  5.9 0.7 copy-start.1
  6.7 0.7 copy-start.3
  6.7 0.7 copy-start.4

commit v5 on v4

--- a/solution.py
+++ b/solution.py
@@ -26,6 +26,8 @@
 
 
 HALF = BLK // 4
+PANEL = 8
+BATCH = 8
 SHIFT = K
 INNER = 2 * K
 WORDS = 2 * HALF
@@ -114,19 +116,26 @@
         half_ref[2 * q + 1] = basis_ref[q, :, BLK:]
     sums_ref[...] = jnp.zeros_like(sums_ref)
 
-    def add_block(n, carry):
-        slot = slot_ref[n]
-        place = slot & (N_COL - 1)
-        side = (slot >> 6) & 3
-        block = tangent_ref[n]
-        none = jnp.zeros_like(block)
-        sides = jnp.concatenate([jnp.where(side == 0, block, none), jnp.where(side == 1, block, none)], axis=0)
-        sums_ref[place] += lax.dot_general(
-            half_ref[slot >> 8], sides, (((1,), (1,)), ((), ())), preferred_element_type=jnp.float32
-        )
+    def add_blocks(step, carry):
+        places, products = [], []
+        for i in range(BATCH):
+            n = step * BATCH + i
+            slot = slot_ref[n]
+            places.append(slot & (N_COL - 1))
+            side = (slot >> 6) & 3
+            block = tangent_ref[n]
+            none = jnp.zeros_like(block)
+            sides = jnp.concatenate([jnp.where(side == 0, block, none), jnp.where(side == 1, block, none)], axis=0)
+            products.append(
+                lax.dot_general(
+                    half_ref[slot >> 8], sides, (((1,), (1,)), ((), ())), preferred_element_type=jnp.float32
+                )
+            )
+        for place, product in zip(places, products):
+            sums_ref[place] += product
         return carry
 
-    lax.fori_loop(0, NNZ, add_block, 0, unroll=8)
+    lax.fori_loop(0, NNZ // BATCH, add_blocks, 0)
     encode(sums_ref, N_COL, out_ref)
 
 
@@ -146,7 +155,7 @@
     )
 
 
-def finish_kernel(gram_ref, product_ref, basis_ref, out_c_ref, out_u_ref, coeff_ref):
+def finish_kernel(gram_ref, product_ref, basis_ref, out_c_ref, out_u_ref, coeff_ref, both_ref):
     packed = gram_ref[...]
     top = pltpu.roll(packed, 16, 1)
     blocks = jnp.concatenate([top, pltpu.roll(packed, 80, 1), packed], axis=0)
@@ -158,22 +167,42 @@
     work = jnp.where(at_lane <= at_row, blocks, below.T[:K])
     work = jnp.where(at_lane == INNER, inner, work)
     work = jnp.where(at_lane == at_row + SHIFT, 1.0, work)
-    for k in range(K - 1):
-        pivot_row = work[k : k + 1, :]
-        factor = work[:, k : k + 1] / pivot_row[:, k : k + 1]
-        work = work - jnp.where(at_row > k, factor * pivot_row, 0.0)
-    pivots = jnp.sum(jnp.where(at_lane == at_row, work, 0.0), axis=1, keepdims=True)
-    work = work / jnp.sqrt(pivots)
+    groups = [work[i : i + 8] for i in range(0, K, 8)]
+    in_group = at_row[:8]
+    pivots = [jnp.ones((8, PAIR), jnp.float32)] * len(groups)
+    for start in range(0, K, PANEL):
+        own = start // 8
+        first = start % 8
+        columns = [
+            [jnp.broadcast_to(group[:, k : k + 1], (8, PAIR)) for group in groups[own:]]
+            for k in range(start, start + PANEL)
+        ]
+        rows = [groups[own][first + i : first + i + 1] for i in range(PANEL)]
+        for i in range(PANEL):
+            pivot = columns[i][0][first + i : first + i + 1]
+            pivots[own] = jnp.where(in_group == first + i, pivot, pivots[own])
+            rows[i] = rows[i] / pivot
+            for j in range(i + 1, PANEL):
+                entry = columns[i][0][first + j : first + j + 1]
+                rows[j] = rows[j] - entry * rows[i]
+                factor = entry / pivot
+                columns[j] = [old - factor * left for old, left in zip(columns[j], columns[i])]
+            columns[i][0] = jnp.where(in_group > first + i, columns[i][0], 0.0)
+        for g in range(own, len(groups)):
+            for i in range(PANEL):
+                groups[g] = groups[g] - columns[i][g - own] * rows[i]
+    work = jnp.concatenate([group / jnp.sqrt(pivot) for group, pivot in zip(groups, pivots)], axis=0)
     inverse = jnp.where((at_lane >= SHIFT) & (at_lane < INNER), work, 0.0)
-
-    def transformed(columns):
-        tall = jnp.concatenate(
-            [jnp.zeros((SHIFT, PAIR), jnp.float32), columns, jnp.zeros((PAIR - INNER, PAIR), jnp.float32)], axis=0
-        )
-        return jnp.dot(inverse, tall, precision=HIGHEST).T.astype(jnp.bfloat16)
-
-    out_c_ref[...] = transformed(product_ref[...])
-    out_u_ref[...] = transformed(basis_ref[...].astype(jnp.float32))
+    columns = jnp.concatenate([product_ref[...], basis_ref[...].astype(jnp.float32)], axis=1)
+    tall = jnp.concatenate(
+        [jnp.zeros((SHIFT, 2 * PAIR), jnp.float32), columns, jnp.zeros((PAIR - INNER, 2 * PAIR), jnp.float32)], axis=0
+    )
+    both_ref[:, :K] = jnp.dot(inverse, tall, precision=HIGHEST).T
+    flat = jnp.concatenate([both_ref[pl.ds(j, 32, stride=8), :][:, :K] for j in range(8)], axis=1)
+    for j in range(8):
+        lanes = slice(8 * K * j, 8 * K * (j + 1))
+        out_c_ref[:, lanes] = jnp.concatenate([flat[j : j + 1], flat[8 + j : 9 + j]], axis=0).astype(jnp.bfloat16)
+        out_u_ref[:, lanes] = jnp.concatenate([flat[16 + j : 17 + j], flat[24 + j : 25 + j]], axis=0).astype(jnp.bfloat16)
     inner = work[:, INNER : INNER + 1] * (1.0 / math.sqrt(TOTAL))
     coeff_ref[...] = jnp.sum(jnp.where(at_lane == at_row, inner, 0.0), axis=0)[:K]
 
@@ -228,21 +257,22 @@
         out_specs=(vmem, vmem),
         compiler_params=params,
     )(far, extra)
-    gram = summed(gram, NEAR, N_NEAR)
-    gram = summed(gram, ROW, N_ROW)
+    gram = summed(gram, ("core",) + NEAR, N_CORE * N_NEAR)
+    gram = summed(gram, "y", N_Y)
     gram = summed(gram, "z_hi", N_Z_HI)
     out_c, out_u, coefficients = pl.pallas_call(
         finish_kernel,
         out_shape=(
-            jax.ShapeDtypeStruct((PAIR, K), jnp.bfloat16),
-            jax.ShapeDtypeStruct((PAIR, K), jnp.bfloat16),
+            jax.ShapeDtypeStruct((2, BLK * K), jnp.bfloat16),
+            jax.ShapeDtypeStruct((2, BLK * K), jnp.bfloat16),
             jax.ShapeDtypeStruct((K,), jnp.float32),
         ),
         in_specs=[vmem, vmem, vmem],
         out_specs=(vmem, vmem, vmem),
+        scratch_shapes=[pltpu.VMEM((2 * PAIR, PAIR), jnp.float32)],
         compiler_params=params,
     )(gram, product, placed)
-    return (out_c.reshape(2, BLK * K), out_u.reshape(2, BLK * K), coefficients)
+    return (out_c, out_u, coefficients)
 
 
 def solution(mesh):

time: 131 us -> 125 us (0.954)
  Pallas kernels: 10.4 us -> 7.95 us
  blocking collectives: 94.3 us -> 91.9 us
  local copies, waits for them, and re-layouts: 5.19 us -> 3.77 us
    pallas_call x1, Pallas kernels: 4.71 us -> 2.23 us  [per_device(): pl.pallas_call(finish_kernel, out_shape=(jax.ShapeDtypeStruct((2, BLK * K...]
    all_to_all x3, blocking collectives: 40.2 us -> 37.8 us  [summed(): return jnp.sum(lax.all_to_all(copies, axes, 0, 0, tiled=True), axis=0)]
    reshape x2 -> x0, local copies, waits for them, and re-layouts: 1.42 us -> none  [per_device(): return (out_c.reshape(2, BLK * K), out_u.reshape(2, BLK * K), coefficients)]
where the time goes in v5:
time: 125 us; the launch traced here: 124 us
  blocking collectives  91.9 us (74%)
  waiting for transfers between devices  14.6 us (12%)
  Pallas kernels  7.95 us (6%)
  starting transfers between devices  3.95 us (3%)
  local copies, waits for them, and re-layouts  3.77 us (3%)
  between operations  1.57 us (1%)
    all_to_all x3, blocking collectives, summed(): return jnp.sum(lax.all_to_all(copies, axes, 0, 0, tiled=True), axis=0)  37.8 us
    all_to_all x1, blocking collectives, per_device(): col_basis = lax.all_to_all(copies, ROW, 0, 0, tiled=True)  18.8 us
    all_to_all x1, blocking collectives, per_device(): near = lax.all_to_all(partial, NEAR, 0, 0, tiled=True)  18 us
    all_to_all x1, blocking collectives, per_device(): far = lax.all_to_all(near, 'z_hi', 0, 0, tiled=True)  17.4 us
    ppermute x1, waiting for transfers between devices, per_device(): lax.ppermute(sideways, COL, [(i, (i + 1) % N_COL) for i in range(N_COL)])  14.6 us
    pallas_call x1, Pallas kernels, per_device(): pl.pallas_call(product_kernel, out_shape=jax.ShapeDtypeStruct((N_COL, WOR...  4.02 us
    ppermute x1, starting transfers between devices, per_device(): lax.ppermute(sideways, COL, [(i, (i + 1) % N_COL) for i in range(N_COL)])  3.95 us
  transfers between devices with their start and end apart: 1, of which 1 were waited for; matrix products, arithmetic and copies ran while one was open for 2% of the time, Pallas kernels for 0%

profile of v5, /device:TPU:1, one launch (start us, length us, event | category | flops | bytes accessed | tf_op | source)
XLA Modules:
  0.0 124.1 jit_solution(11924564195558730585)
XLA Ops:
  0.6 0.0 copy-start.2
  0.6 0.0 copy-start
  0.7 0.6 copy-done.2
  1.4 0.0 copy-done
  1.4 0.1 fusion
  1.5 0.1 select_n.44
  1.6 0.1 copy.12
  1.7 0.1 select_n.47
  1.8 0.1 copy.13
  1.9 0.1 pad_maximum_fusion
  2.0 4.0 %collective-permute-start = (bf16[48,128]{1,0:T(8,128)(2,1)S(1)}, bf16[48,128]{1,0:T(8,128)(2,1)S(1)}, u32[]{:S(2)}, u32[]{:S(2)}) collective-permute-start(bf16[48,128]{1,0:T(8,128)(2,1)S(1)} %pad_maximum_fusion), channel_id=1, source_target_pairs={{0,1},{1,2},{2,3},{3,4},{4,5},{5,6},{6,7},{7,8},{8,9},{9,10},{10,1... | collective-permute-start | bytes 36872 | tf_op jit(solution)/shard_map/ppermute | solution.py:222
  5.9 0.0 copy-start.1
  6.6 0.0 copy-done.1
  6.6 0.1 broadcast_select_fusion.2.extra_ref
  6.7 0.0 copy-start.3
  6.7 0.0 copy-start.4
  6.7 0.6 copy-done.3
  7.4 0.0 copy-done.4
  7.4 2.1 %reshape.39.tangent_ref = bf16[64,64,64]{2,1,0:T(8,128)(2,1)S(1)} reshape(bf16[1,1,64,4096]{3,2,1,0:T(8,128)(2,1)} %param.7) | data formatting | bytes 1048576 | tf_op jit(solution)/shard_map/reshape | solution.py:229
  9.4 14.6 %collective-permute-done.basis_ref = bf16[48,128]{1,0:T(8,128)(2,1)S(1)} collective-permute-done((bf16[48,128]{1,0:T(8,128)(2,1)S(1)}, bf16[48,128]{1,0:T(8,128)(2,1)S(1)}, u32[]{:S(2)}, u32[]{:S(2)}) %collective-permute-start) | collective-permute-done | bytes 12320 | tf_op jit(solution)/shard_map/ppermute | solution.py:222
  24.0 18.8 %all_to_all.30.basis_ref = bf16[16,48,128]{2,1,0:T(8,128)(2,1)S(1)} all-to-all(bf16[16,48,128]{2,1,0:T(8,128)(2,1)S(1)} %broadcast_in_dim.43), channel_id=1, replica_groups=mesh['y'=8,'core'=2,'z_hi'=8,'z_lo'=2,'x'=4] {'y','core'}, dimensions={0} | all-to-all | bytes 393216 | tf_op jit(solution)/shard_map/all_to_all | solution.py:231
  42.8 4.0 %shard_map.94 = s32[64,32,128]{2,1,0:T(8,128)S(1)} custom-call(s32[64]{0:T(128)S(1)} %bitcast_add_fusion.slot_ref, bf16[64,64,64]{2,1,0:T(8,128)(2,1)S(1)} %reshape.39.tangent_ref, bf16[16,48,128]{2,1,0:T(8,128)(2,1)S(1)} %all_to_all.30.basis_ref), custom_call_target="tpu_custom_call" | custom-call | tf_op jit(solution)/shard_map/pallas_call | solution.py:232
  46.8 18.0 %all_to_all.31 = s32[64,32,128]{2,1,0:T(8,128)S(1)} all-to-all(s32[64,32,128]{2,1,0:T(8,128)S(1)} %shard_map.94), channel_id=1, replica_groups=mesh['y'=8,'core'=2,'z_hi'=8,'z_lo'=2,'x'=4] {'z_lo','x'}, dimensions={0} | all-to-all | bytes 2097152 | tf_op jit(solution)/shard_map/all_to_all | solution.py:240
  64.8 1.0 shard_map.95
  65.8 17.4 %all_to_all.32.far_ref = s32[8,32,128]{2,1,0:T(8,128)S(1)} all-to-all(s32[8,32,128]{2,1,0:T(8,128)S(1)} %shard_map.95), channel_id=1, replica_groups=mesh['y'=8,'core'=2,'z_hi'=8,'z_lo'=2,'x'=4] {'z_hi'}, dimensions={0} | all-to-all | bytes 262144 | tf_op jit(solution)/shard_map/all_to_all | solution.py:249
  83.1 0.7 shard_map.96
  83.9 13.6 %all_to_all.33 = f32[16,16,128]{2,1,0:T(8,128)S(1)} all-to-all(f32[16,16,128]{2,1,0:T(8,128)S(1)} %broadcast_in_dim.44), channel_id=1, replica_groups=mesh['y'=8,'core'=2,'z_hi'=8,'z_lo'=2,'x'=4] {'core','z_lo','x'}, dimensions={0} | all-to-all | bytes 262144 | tf_op jit(solution)/shard_map/all_to_all | solution.py:212
  97.5 9.5 %all_to_all.34 = f32[8,16,128]{2,1,0:T(8,128)S(1)} all-to-all(f32[8,16,128]{2,1,0:T(8,128)S(1)} %broadcast_in_dim.45), channel_id=1, replica_groups=mesh['y'=8,'core'=2,'z_hi'=8,'z_lo'=2,'x'=4] {'y'}, dimensions={0} | all-to-all | bytes 131072 | tf_op jit(solution)/shard_map/all_to_all | solution.py:212
  107.1 14.7 %all_to_all.35 = f32[8,16,128]{2,1,0:T(8,128)S(1)} all-to-all(f32[8,16,128]{2,1,0:T(8,128)S(1)} %broadcast_in_dim.46), channel_id=1, replica_groups=mesh['y'=8,'core'=2,'z_hi'=8,'z_lo'=2,'x'=4] {'z_hi'}, dimensions={0} | all-to-all | bytes 131072 | tf_op jit(solution)/shard_map/all_to_all | solution.py:212
  121.8 2.2 %shard_map.97 = (bf16[2,3072]{1,0:T(2,128)(2,1)}, bf16[2,3072]{1,0:T(2,128)(2,1)}, f32[48]{0:T(128)}) custom-call(f32[16,128]{1,0:T(8,128)S(1)} %reduce_sum.29.gram_ref, f32[48,128]{1,0:T(8,128)S(1)} %get-tuple-element.14.product_ref, bf16[48,128]{1,0:T(8,128)(2,1)S(1)} %collective-permute-done.basis_ref), custom_call_target="tpu_custom_call" | custom-call | tf_op jit(solution)/shard_map/pallas_call | solution.py:263
  (9 shorter events, 0.1 us)
Async XLA Ops:
  0.6 0.7 copy-start.2
  0.6 0.8 copy-start
  2.0 22.0 %collective-permute-start = (bf16[48,128]{1,0:T(8,128)(2,1)S(1)}, bf16[48,128]{1,0:T(8,128)(2,1)S(1)}, u32[]{:S(2)}, u32[]{:S(2)}) collective-permute-start(bf16[48,128]{1,0:T(8,128)(2,1)S(1)} %pad_maximum_fusion), channel_id=1, source_target_pairs={{0,1},{1,2},{2,3},{3,4},{4,5},{5,6},{6,7},{7,8},{8,9},{9,10},{10,1... | collective-permute-start | bytes 36872 | tf_op jit(solution)/shard_map/ppermute | solution.py:222
  5.9 0.7 copy-start.1
  6.7 0.7 copy-start.3
  6.7 0.7 copy-start.4

commit v6 on v5

--- a/solution.py
+++ b/solution.py
@@ -27,7 +27,7 @@
 
 HALF = BLK // 4
 PANEL = 8
-BATCH = 8
+BATCH = 64
 SHIFT = K
 INNER = 2 * K
 WORDS = 2 * HALF
@@ -40,7 +40,7 @@
     def look(i, peak):
         return jnp.maximum(peak, jnp.abs(sums_ref[i]))
 
-    peak = lax.fori_loop(0, count, look, jnp.zeros((K, PAIR), jnp.float32), unroll=8)
+    peak = lax.fori_loop(0, count, look, jnp.zeros((K, PAIR), jnp.float32), unroll=min(count, 16))
     peak = jnp.broadcast_to(jnp.max(peak, axis=1, keepdims=True), (K, PAIR))
     factor = jnp.full((K, PAIR), 2.0**19, jnp.float32)
     power = jnp.zeros((K, PAIR), jnp.int32)
@@ -67,7 +67,7 @@
         out_ref[i, HALF:] = (code[HALF:WORDS] << 11) | (third & 0x3FF) | flags
         return carry
 
-    lax.fori_loop(0, count, put, 0, unroll=8)
+    lax.fori_loop(0, count, put, 0, unroll=min(count, 16))
 
 
 def unit_of(second):
@@ -99,14 +99,11 @@
     for source in range(N_NEAR):
         unit_ref[source] = unit_of(near_ref[source, 0, HALF:])
 
-    def add(i, carry):
+    for i in range(N_Z_HI):
         total = decode(near_ref[0, i]) * unit_ref[0]
         for source in range(1, N_NEAR):
             total += decode(near_ref[source, i]) * unit_ref[source]
         sums_ref[i] = total
-        return carry
-
-    lax.fori_loop(0, N_Z_HI, add, 0)
     encode(sums_ref, N_Z_HI, out_ref)
 
 
@@ -115,6 +112,8 @@
         half_ref[2 * q] = basis_ref[q, :, :BLK]
         half_ref[2 * q + 1] = basis_ref[q, :, BLK:]
     sums_ref[...] = jnp.zeros_like(sums_ref)
+
+    side_of_lane = lax.broadcasted_iota(jnp.int32, (K, PAIR), 1) >> 6
 
     def add_blocks(step, carry):
         places, products = [], []
@@ -123,14 +122,10 @@
             slot = slot_ref[n]
             places.append(slot & (N_COL - 1))
             side = (slot >> 6) & 3
-            block = tangent_ref[n]
-            none = jnp.zeros_like(block)
-            sides = jnp.concatenate([jnp.where(side == 0, block, none), jnp.where(side == 1, block, none)], axis=0)
-            products.append(
-                lax.dot_general(
-                    half_ref[slot >> 8], sides, (((1,), (1,)), ((), ())), preferred_element_type=jnp.float32
-                )
+            product = lax.dot_general(
+                half_ref[slot >> 8], tangent_ref[n], (((1,), (1,)), ((), ())), preferred_element_type=jnp.float32
             )
+            products.append(jnp.where(side_of_lane == side, jnp.concatenate([product, product], axis=1), 0.0))
         for place, product in zip(places, products):
             sums_ref[place] += product
         return carry

time: 125 us -> 123 us (0.984)
  Pallas kernels: 7.95 us -> 6.12 us
    pallas_call x1, Pallas kernels: 4.02 us -> 2.32 us  [per_device(): pl.pallas_call(product_kernel, out_shape=jax.ShapeDtypeStruct((N_COL, WOR...]
where the time goes in v6:
time: 123 us; the launch traced here: 122 us
  blocking collectives  91.9 us (75%)
  waiting for transfers between devices  14.6 us (12%)
  Pallas kernels  6.12 us (5%)
  starting transfers between devices  3.95 us (3%)
  local copies, waits for them, and re-layouts  3.77 us (3%)
  between operations  1.57 us (1%)
    all_to_all x3, blocking collectives, summed(): return jnp.sum(lax.all_to_all(copies, axes, 0, 0, tiled=True), axis=0)  37.8 us
    all_to_all x1, blocking collectives, per_device(): col_basis = lax.all_to_all(copies, ROW, 0, 0, tiled=True)  18.8 us
    all_to_all x1, blocking collectives, per_device(): near = lax.all_to_all(partial, NEAR, 0, 0, tiled=True)  18 us
    all_to_all x1, blocking collectives, per_device(): far = lax.all_to_all(near, 'z_hi', 0, 0, tiled=True)  17.4 us
    ppermute x1, waiting for transfers between devices, per_device(): lax.ppermute(sideways, COL, [(i, (i + 1) % N_COL) for i in range(N_COL)])  14.6 us
    ppermute x1, starting transfers between devices, per_device(): lax.ppermute(sideways, COL, [(i, (i + 1) % N_COL) for i in range(N_COL)])  3.95 us
  transfers between devices with their start and end apart: 1, of which 1 were waited for; matrix products, arithmetic and copies ran while one was open for 2% of the time, Pallas kernels for 0%

profile of v6, /device:TPU:1, one launch (start us, length us, event | category | flops | bytes accessed | tf_op | source)
XLA Modules:
  0.0 122.2 jit_solution(12271622229106484120)
XLA Ops:
  0.6 0.0 copy-start.2
  0.6 0.0 copy-start
  0.7 0.6 copy-done.2
  1.4 0.0 copy-done
  1.4 0.1 fusion
  1.5 0.1 select_n.44
  1.6 0.1 copy.12
  1.7 0.1 select_n.47
  1.8 0.1 copy.13
  1.9 0.1 pad_maximum_fusion
  2.0 4.0 %collective-permute-start = (bf16[48,128]{1,0:T(8,128)(2,1)S(1)}, bf16[48,128]{1,0:T(8,128)(2,1)S(1)}, u32[]{:S(2)}, u32[]{:S(2)}) collective-permute-start(bf16[48,128]{1,0:T(8,128)(2,1)S(1)} %pad_maximum_fusion), channel_id=1, source_target_pairs={{0,1},{1,2},{2,3},{3,4},{4,5},{5,6},{6,7},{7,8},{8,9},{9,10},{10,1... | collective-permute-start | bytes 36872 | tf_op jit(solution)/shard_map/ppermute | solution.py:217
  5.9 0.0 copy-start.1
  6.6 0.0 copy-done.1
  6.6 0.1 broadcast_select_fusion.2.extra_ref
  6.7 0.0 copy-start.3
  6.7 0.0 copy-start.4
  6.7 0.6 copy-done.3
  7.4 0.0 copy-done.4
  7.4 2.1 %reshape.39.tangent_ref = bf16[64,64,64]{2,1,0:T(8,128)(2,1)S(1)} reshape(bf16[1,1,64,4096]{3,2,1,0:T(8,128)(2,1)} %param.7) | data formatting | bytes 1048576 | tf_op jit(solution)/shard_map/reshape | solution.py:224
  9.4 14.6 %collective-permute-done.basis_ref = bf16[48,128]{1,0:T(8,128)(2,1)S(1)} collective-permute-done((bf16[48,128]{1,0:T(8,128)(2,1)S(1)}, bf16[48,128]{1,0:T(8,128)(2,1)S(1)}, u32[]{:S(2)}, u32[]{:S(2)}) %collective-permute-start) | collective-permute-done | bytes 12320 | tf_op jit(solution)/shard_map/ppermute | solution.py:217
  24.0 18.8 %all_to_all.30.basis_ref = bf16[16,48,128]{2,1,0:T(8,128)(2,1)S(1)} all-to-all(bf16[16,48,128]{2,1,0:T(8,128)(2,1)S(1)} %broadcast_in_dim.43), channel_id=1, replica_groups=mesh['y'=8,'core'=2,'z_hi'=8,'z_lo'=2,'x'=4] {'y','core'}, dimensions={0} | all-to-all | bytes 393216 | tf_op jit(solution)/shard_map/all_to_all | solution.py:226
  42.8 2.3 %shard_map.94 = s32[64,32,128]{2,1,0:T(8,128)S(1)} custom-call(s32[64]{0:T(128)S(1)} %bitcast_add_fusion.slot_ref, bf16[64,64,64]{2,1,0:T(8,128)(2,1)S(1)} %reshape.39.tangent_ref, bf16[16,48,128]{2,1,0:T(8,128)(2,1)S(1)} %all_to_all.30.basis_ref), custom_call_target="tpu_custom_call" | custom-call | tf_op jit(solution)/shard_map/pallas_call | solution.py:227
  45.1 18.0 %all_to_all.31 = s32[64,32,128]{2,1,0:T(8,128)S(1)} all-to-all(s32[64,32,128]{2,1,0:T(8,128)S(1)} %shard_map.94), channel_id=1, replica_groups=mesh['y'=8,'core'=2,'z_hi'=8,'z_lo'=2,'x'=4] {'z_lo','x'}, dimensions={0} | all-to-all | bytes 2097152 | tf_op jit(solution)/shard_map/all_to_all | solution.py:235
  63.1 0.8 shard_map.95
  64.0 17.4 %all_to_all.32.far_ref = s32[8,32,128]{2,1,0:T(8,128)S(1)} all-to-all(s32[8,32,128]{2,1,0:T(8,128)S(1)} %shard_map.95), channel_id=1, replica_groups=mesh['y'=8,'core'=2,'z_hi'=8,'z_lo'=2,'x'=4] {'z_hi'}, dimensions={0} | all-to-all | bytes 262144 | tf_op jit(solution)/shard_map/all_to_all | solution.py:244
  81.3 0.7 shard_map.96
  82.1 13.6 %all_to_all.33 = f32[16,16,128]{2,1,0:T(8,128)S(1)} all-to-all(f32[16,16,128]{2,1,0:T(8,128)S(1)} %broadcast_in_dim.44), channel_id=1, replica_groups=mesh['y'=8,'core'=2,'z_hi'=8,'z_lo'=2,'x'=4] {'core','z_lo','x'}, dimensions={0} | all-to-all | bytes 262144 | tf_op jit(solution)/shard_map/all_to_all | solution.py:207
  95.7 9.5 %all_to_all.34 = f32[8,16,128]{2,1,0:T(8,128)S(1)} all-to-all(f32[8,16,128]{2,1,0:T(8,128)S(1)} %broadcast_in_dim.45), channel_id=1, replica_groups=mesh['y'=8,'core'=2,'z_hi'=8,'z_lo'=2,'x'=4] {'y'}, dimensions={0} | all-to-all | bytes 131072 | tf_op jit(solution)/shard_map/all_to_all | solution.py:207
  105.2 14.7 %all_to_all.35 = f32[8,16,128]{2,1,0:T(8,128)S(1)} all-to-all(f32[8,16,128]{2,1,0:T(8,128)S(1)} %broadcast_in_dim.46), channel_id=1, replica_groups=mesh['y'=8,'core'=2,'z_hi'=8,'z_lo'=2,'x'=4] {'z_hi'}, dimensions={0} | all-to-all | bytes 131072 | tf_op jit(solution)/shard_map/all_to_all | solution.py:207
  120.0 2.2 %shard_map.97 = (bf16[2,3072]{1,0:T(2,128)(2,1)}, bf16[2,3072]{1,0:T(2,128)(2,1)}, f32[48]{0:T(128)}) custom-call(f32[16,128]{1,0:T(8,128)S(1)} %reduce_sum.29.gram_ref, f32[48,128]{1,0:T(8,128)S(1)} %get-tuple-element.14.product_ref, bf16[48,128]{1,0:T(8,128)(2,1)S(1)} %collective-permute-done.basis_ref), custom_call_target="tpu_custom_call" | custom-call | tf_op jit(solution)/shard_map/pallas_call | solution.py:258
  (9 shorter events, 0.1 us)
Async XLA Ops:
  0.6 0.7 copy-start.2
  0.6 0.8 copy-start
  2.0 22.0 %collective-permute-start = (bf16[48,128]{1,0:T(8,128)(2,1)S(1)}, bf16[48,128]{1,0:T(8,128)(2,1)S(1)}, u32[]{:S(2)}, u32[]{:S(2)}) collective-permute-start(bf16[48,128]{1,0:T(8,128)(2,1)S(1)} %pad_maximum_fusion), channel_id=1, source_target_pairs={{0,1},{1,2},{2,3},{3,4},{4,5},{5,6},{6,7},{7,8},{8,9},{9,10},{10,1... | collective-permute-start | bytes 36872 | tf_op jit(solution)/shard_map/ppermute | solution.py:217
  5.9 0.7 copy-start.1
  6.7 0.7 copy-start.3
  6.7 0.7 copy-start.4

commit v7 on v6

--- a/solution.py
+++ b/solution.py
@@ -141,22 +141,32 @@
     product_ref[...] = product
     both = jnp.concatenate([product, extra_ref[...]], axis=0)
     gram = lax.dot_general(product, both, (((1,), (1,)), ((), ())), precision=HIGHEST)
+    row = lax.broadcasted_iota(jnp.int32, (HALF, PAIR), 0)
     lane = lax.broadcasted_iota(jnp.int32, (HALF, PAIR), 1)
+
+    def by_lane(bottom, middle, top):
+        return jnp.where(lane < K, bottom, jnp.where(lane < 80, middle, top))
+
     top, middle, bottom = gram[:HALF], gram[HALF:WORDS], gram[WORDS:]
-    gram_ref[...] = jnp.where(
-        (lane < K) | (lane == 96),
-        bottom,
-        jnp.where((lane < 80) | (lane == 97), pltpu.roll(middle, 48, 1), pltpu.roll(top, 112, 1)),
-    )
+    packed = by_lane(bottom, pltpu.roll(middle, K, 1), pltpu.roll(top, 80, 1))
+    inner = by_lane(*(jnp.broadcast_to(part[:, INNER : INNER + 1], (HALF, PAIR)) for part in (bottom, middle, top)))
+    place = lane - by_lane(32, 64, 80)
+    packed = jnp.where(place == row + 1, inner, packed)
+    packed = jnp.where((place == 2) & (row == 0), inner[HALF - 1 :], packed)
+    gram_ref[...] = jnp.concatenate([packed[i : i + 4, : 2 * K] for i in range(0, HALF, 4)], axis=1)
 
 
 def finish_kernel(gram_ref, product_ref, basis_ref, out_c_ref, out_u_ref, coeff_ref, both_ref):
-    packed = gram_ref[...]
-    top = pltpu.roll(packed, 16, 1)
-    blocks = jnp.concatenate([top, pltpu.roll(packed, 80, 1), packed], axis=0)
-    inner = jnp.concatenate([top, pltpu.roll(packed, 127, 1), packed], axis=0)
+    wide = gram_ref[...]
+    packed = jnp.concatenate([wide[:, 2 * K * i : 2 * K * (i + 1)] for i in range(4)], axis=0)
+    packed = jnp.concatenate([packed, jnp.zeros((HALF, PAIR - 2 * K), jnp.float32)], axis=1)
+    blocks = jnp.concatenate([pltpu.roll(packed, K, 1), pltpu.roll(packed, 80, 1), packed], axis=0)
     at_row = lax.broadcasted_iota(jnp.int32, (K, PAIR), 0)
     at_lane = lax.broadcasted_iota(jnp.int32, (K, PAIR), 1)
+    inner = jnp.sum(jnp.where(at_lane == at_row + 1, blocks, 0.0), axis=1, keepdims=True)
+    last = jnp.sum(jnp.where(at_lane == at_row + 2, blocks, 0.0), axis=1, keepdims=True)
+    last = jnp.concatenate([jnp.broadcast_to(last[i : i + 1], (HALF, 1)) for i in range(0, K, HALF)], axis=0)
+    inner = jnp.where((at_row & (HALF - 1)) == HALF - 1, last, inner)
     blocks = blocks * (1.0 / TOTAL)
     below = jnp.concatenate([jnp.where(at_lane < at_row, blocks, 0.0), jnp.zeros((PAIR - K, PAIR), jnp.float32)], axis=0)
     work = jnp.where(at_lane <= at_row, blocks, below.T[:K])
@@ -176,11 +186,12 @@
         for i in range(PANEL):
             pivot = columns[i][0][first + i : first + i + 1]
             pivots[own] = jnp.where(in_group == first + i, pivot, pivots[own])
-            rows[i] = rows[i] / pivot
+            inverse = 1.0 / pivot
+            rows[i] = rows[i] * inverse
             for j in range(i + 1, PANEL):
                 entry = columns[i][0][first + j : first + j + 1]
                 rows[j] = rows[j] - entry * rows[i]
-                factor = entry / pivot
+                factor = entry * inverse
                 columns[j] = [old - factor * left for old, left in zip(columns[j], columns[i])]
             columns[i][0] = jnp.where(in_group > first + i, columns[i][0], 0.0)
         for g in range(own, len(groups)):
@@ -220,7 +231,7 @@
     side = jnp.where(jnp.arange(NNZ) < tile_count.reshape(1), rows & 1, 2)
     slots = (owner & (N_NEAR - 1)) * N_Z_HI + (owner >> 3) + (side << 6) + (cols << 8)
     at_row = lax.broadcasted_iota(jnp.int32, (PAIR - K, PAIR), 0)
-    extra = jnp.where((at_row == 1) | (at_row == K), residual.reshape(1, PAIR), 0.0)
+    extra = jnp.where(at_row == K, residual.reshape(1, PAIR), 0.0)
     blocks, slots, extra, sent = lax.optimization_barrier((tangent.reshape(NNZ, BLK, BLK), slots, extra, placed))
     copies = jnp.broadcast_to(sent[None], (N_ROW, K, PAIR))
     col_basis = lax.all_to_all(copies, ROW, 0, 0, tiled=True)
@@ -246,15 +257,15 @@
         gram_kernel,
         out_shape=(
             jax.ShapeDtypeStruct((K, PAIR), jnp.float32),
-            jax.ShapeDtypeStruct((HALF, PAIR), jnp.float32),
+            jax.ShapeDtypeStruct((4, 4 * 2 * K), jnp.float32),
         ),
         in_specs=[vmem, vmem],
         out_specs=(vmem, vmem),
         compiler_params=params,
     )(far, extra)
     gram = summed(gram, ("core",) + NEAR, N_CORE * N_NEAR)
+    gram = summed(gram, "z_hi", N_Z_HI)
     gram = summed(gram, "y", N_Y)
-    gram = summed(gram, "z_hi", N_Z_HI)
     out_c, out_u, coefficients = pl.pallas_call(
         finish_kernel,
         out_shape=(

time: 123 us -> 123 us (level)
  no operation moved by 1% of the time
where the time goes in v7:
time: 123 us; the launch traced here: 122 us
  blocking collectives  91.4 us (74%)
  waiting for transfers between devices  14.6 us (12%)
  Pallas kernels  6.4 us (5%)
  starting transfers between devices  3.95 us (3%)
  local copies, waits for them, and re-layouts  3.78 us (3%)
  between operations  1.55 us (1%)
    all_to_all x3, blocking collectives, summed(): return jnp.sum(lax.all_to_all(copies, axes, 0, 0, tiled=True), axis=0)  37.3 us
    all_to_all x1, blocking collectives, per_device(): col_basis = lax.all_to_all(copies, ROW, 0, 0, tiled=True)  18.8 us
    all_to_all x1, blocking collectives, per_device(): near = lax.all_to_all(partial, NEAR, 0, 0, tiled=True)  18 us
    all_to_all x1, blocking collectives, per_device(): far = lax.all_to_all(near, 'z_hi', 0, 0, tiled=True)  17.4 us
    ppermute x1, waiting for transfers between devices, per_device(): lax.ppermute(sideways, COL, [(i, (i + 1) % N_COL) for i in range(N_COL)])  14.6 us
    ppermute x1, starting transfers between devices, per_device(): lax.ppermute(sideways, COL, [(i, (i + 1) % N_COL) for i in range(N_COL)])  3.95 us
  transfers between devices with their start and end apart: 1, of which 1 were waited for; matrix products, arithmetic and copies ran while one was open for 2% of the time, Pallas kernels for 0%

profile of v7, /device:TPU:1, one launch (start us, length us, event | category | flops | bytes accessed | tf_op | source)
XLA Modules:
  0.0 122.0 jit_solution(1571263566533724770)
XLA Ops:
  0.6 0.0 copy-start.2
  0.6 0.0 copy-start
  0.7 0.6 copy-done.2
  1.4 0.0 copy-done
  1.4 0.1 fusion
  1.5 0.1 select_n.44
  1.6 0.1 copy.14
  1.7 0.1 select_n.47
  1.8 0.1 copy.15
  1.9 0.1 pad_maximum_fusion
  2.0 4.0 %collective-permute-start = (bf16[48,128]{1,0:T(8,128)(2,1)S(1)}, bf16[48,128]{1,0:T(8,128)(2,1)S(1)}, u32[]{:S(2)}, u32[]{:S(2)}) collective-permute-start(bf16[48,128]{1,0:T(8,128)(2,1)S(1)} %pad_maximum_fusion), channel_id=1, source_target_pairs={{0,1},{1,2},{2,3},{3,4},{4,5},{5,6},{6,7},{7,8},{8,9},{9,10},{10,1... | collective-permute-start | bytes 36872 | tf_op jit(solution)/shard_map/ppermute | solution.py:228
  5.9 0.0 copy-start.1
  6.6 0.0 copy-done.1
  6.6 0.1 broadcast_select_fusion.2.extra_ref
  6.7 0.0 copy-start.3
  6.7 0.0 copy-start.4
  6.7 0.6 copy-done.3
  7.4 0.0 copy-done.4
  7.4 2.1 %reshape.39.tangent_ref = bf16[64,64,64]{2,1,0:T(8,128)(2,1)S(1)} reshape(bf16[1,1,64,4096]{3,2,1,0:T(8,128)(2,1)} %param.7) | data formatting | bytes 1048576 | tf_op jit(solution)/shard_map/reshape | solution.py:235
  9.4 14.6 %collective-permute-done.basis_ref = bf16[48,128]{1,0:T(8,128)(2,1)S(1)} collective-permute-done((bf16[48,128]{1,0:T(8,128)(2,1)S(1)}, bf16[48,128]{1,0:T(8,128)(2,1)S(1)}, u32[]{:S(2)}, u32[]{:S(2)}) %collective-permute-start) | collective-permute-done | bytes 12320 | tf_op jit(solution)/shard_map/ppermute | solution.py:228
  24.0 18.8 %all_to_all.30.basis_ref = bf16[16,48,128]{2,1,0:T(8,128)(2,1)S(1)} all-to-all(bf16[16,48,128]{2,1,0:T(8,128)(2,1)S(1)} %broadcast_in_dim.43), channel_id=1, replica_groups=mesh['y'=8,'core'=2,'z_hi'=8,'z_lo'=2,'x'=4] {'y','core'}, dimensions={0} | all-to-all | bytes 393216 | tf_op jit(solution)/shard_map/all_to_all | solution.py:237
  42.8 2.3 %shard_map.94 = s32[64,32,128]{2,1,0:T(8,128)S(1)} custom-call(s32[64]{0:T(128)S(1)} %bitcast_add_fusion.slot_ref, bf16[64,64,64]{2,1,0:T(8,128)(2,1)S(1)} %reshape.39.tangent_ref, bf16[16,48,128]{2,1,0:T(8,128)(2,1)S(1)} %all_to_all.30.basis_ref), custom_call_target="tpu_custom_call" | custom-call | tf_op jit(solution)/shard_map/pallas_call | solution.py:238
  45.1 18.0 %all_to_all.31 = s32[64,32,128]{2,1,0:T(8,128)S(1)} all-to-all(s32[64,32,128]{2,1,0:T(8,128)S(1)} %shard_map.94), channel_id=1, replica_groups=mesh['y'=8,'core'=2,'z_hi'=8,'z_lo'=2,'x'=4] {'z_lo','x'}, dimensions={0} | all-to-all | bytes 2097152 | tf_op jit(solution)/shard_map/all_to_all | solution.py:246
  63.1 0.8 shard_map.95
  64.0 17.4 %all_to_all.32.far_ref = s32[8,32,128]{2,1,0:T(8,128)S(1)} all-to-all(s32[8,32,128]{2,1,0:T(8,128)S(1)} %shard_map.95), channel_id=1, replica_groups=mesh['y'=8,'core'=2,'z_hi'=8,'z_lo'=2,'x'=4] {'z_hi'}, dimensions={0} | all-to-all | bytes 262144 | tf_op jit(solution)/shard_map/all_to_all | solution.py:255
  81.3 0.8 shard_map.96
  82.2 13.2 %all_to_all.33 = f32[16,4,384]{2,1,0:T(4,128)S(1)} all-to-all(f32[16,4,384]{2,1,0:T(4,128)S(1)} %broadcast_in_dim.44), channel_id=1, replica_groups=mesh['y'=8,'core'=2,'z_hi'=8,'z_lo'=2,'x'=4] {'core','z_lo','x'}, dimensions={0} | all-to-all | bytes 196608 | tf_op jit(solution)/shard_map/all_to_all | solution.py:218
  95.4 14.5 %all_to_all.34 = f32[8,4,384]{2,1,0:T(4,128)S(1)} all-to-all(f32[8,4,384]{2,1,0:T(4,128)S(1)} %broadcast_in_dim.45), channel_id=1, replica_groups=mesh['y'=8,'core'=2,'z_hi'=8,'z_lo'=2,'x'=4] {'z_hi'}, dimensions={0} | all-to-all | bytes 98304 | tf_op jit(solution)/shard_map/all_to_all | solution.py:218
  110.0 9.5 %all_to_all.35 = f32[8,4,384]{2,1,0:T(4,128)S(1)} all-to-all(f32[8,4,384]{2,1,0:T(4,128)S(1)} %broadcast_in_dim.46), channel_id=1, replica_groups=mesh['y'=8,'core'=2,'z_hi'=8,'z_lo'=2,'x'=4] {'y'}, dimensions={0} | all-to-all | bytes 98304 | tf_op jit(solution)/shard_map/all_to_all | solution.py:218
  119.6 2.4 %shard_map.97 = (bf16[2,3072]{1,0:T(2,128)(2,1)}, bf16[2,3072]{1,0:T(2,128)(2,1)}, f32[48]{0:T(128)}) custom-call(f32[4,384]{1,0:T(4,128)S(1)} %reduce_sum.29.gram_ref, f32[48,128]{1,0:T(8,128)S(1)} %get-tuple-element.14.product_ref, bf16[48,128]{1,0:T(8,128)(2,1)S(1)} %collective-permute-done.basis_ref), custom_call_target="tpu_custom_call" | custom-call | tf_op jit(solution)/shard_map/pallas_call | solution.py:269
  (9 shorter events, 0.2 us)
Async XLA Ops:
  0.6 0.7 copy-start.2
  0.6 0.8 copy-start
  2.0 22.0 %collective-permute-start = (bf16[48,128]{1,0:T(8,128)(2,1)S(1)}, bf16[48,128]{1,0:T(8,128)(2,1)S(1)}, u32[]{:S(2)}, u32[]{:S(2)}) collective-permute-start(bf16[48,128]{1,0:T(8,128)(2,1)S(1)} %pad_maximum_fusion), channel_id=1, source_target_pairs={{0,1},{1,2},{2,3},{3,4},{4,5},{5,6},{6,7},{7,8},{8,9},{9,10},{10,1... | collective-permute-start | bytes 36872 | tf_op jit(solution)/shard_map/ppermute | solution.py:228
  5.9 0.7 copy-start.1
  6.7 0.7 copy-start.3
  6.7 0.7 copy-start.4

commit v8 on v7

--- a/solution.py
+++ b/solution.py
@@ -40,7 +40,7 @@
     def look(i, peak):
         return jnp.maximum(peak, jnp.abs(sums_ref[i]))
 
-    peak = lax.fori_loop(0, count, look, jnp.zeros((K, PAIR), jnp.float32), unroll=min(count, 16))
+    peak = lax.fori_loop(0, count, look, jnp.zeros((K, PAIR), jnp.float32), unroll=count)
     peak = jnp.broadcast_to(jnp.max(peak, axis=1, keepdims=True), (K, PAIR))
     factor = jnp.full((K, PAIR), 2.0**19, jnp.float32)
     power = jnp.zeros((K, PAIR), jnp.int32)
@@ -67,7 +67,7 @@
         out_ref[i, HALF:] = (code[HALF:WORDS] << 11) | (third & 0x3FF) | flags
         return carry
 
-    lax.fori_loop(0, count, put, 0, unroll=min(count, 16))
+    lax.fori_loop(0, count, put, 0, unroll=count)
 
 
 def unit_of(second):
@@ -263,8 +263,8 @@
         out_specs=(vmem, vmem),
         compiler_params=params,
     )(far, extra)
-    gram = summed(gram, ("core",) + NEAR, N_CORE * N_NEAR)
-    gram = summed(gram, "z_hi", N_Z_HI)
+    gram = summed(gram, ("core", "x"), N_CORE * N_X)
+    gram = summed(gram, ("z_hi", "z_lo"), N_Z_HI * N_Z_LO)
     gram = summed(gram, "y", N_Y)
     out_c, out_u, coefficients = pl.pallas_call(
         finish_kernel,

time: 123 us -> 122 us (level)
  no operation moved by 1% of the time
where the time goes in v8:
time: 122 us; the launch traced here: 121 us
  blocking collectives  90.2 us (74%)
  waiting for transfers between devices  14.6 us (12%)
  Pallas kernels  6.33 us (5%)
  starting transfers between devices  3.95 us (3%)
  local copies, waits for them, and re-layouts  3.78 us (3%)
  between operations  1.55 us (1%)
    all_to_all x3, blocking collectives, summed(): return jnp.sum(lax.all_to_all(copies, axes, 0, 0, tiled=True), axis=0)  36.1 us
    all_to_all x1, blocking collectives, per_device(): col_basis = lax.all_to_all(copies, ROW, 0, 0, tiled=True)  18.8 us
    all_to_all x1, blocking collectives, per_device(): near = lax.all_to_all(partial, NEAR, 0, 0, tiled=True)  18 us
    all_to_all x1, blocking collectives, per_device(): far = lax.all_to_all(near, 'z_hi', 0, 0, tiled=True)  17.4 us
    ppermute x1, waiting for transfers between devices, per_device(): lax.ppermute(sideways, COL, [(i, (i + 1) % N_COL) for i in range(N_COL)])  14.6 us
    ppermute x1, starting transfers between devices, per_device(): lax.ppermute(sideways, COL, [(i, (i + 1) % N_COL) for i in range(N_COL)])  3.95 us
    pallas_call x1, Pallas kernels, per_device(): pl.pallas_call(finish_kernel, out_shape=(jax.ShapeDtypeStruct((2, BLK * K...  2.44 us
  transfers between devices with their start and end apart: 1, of which 1 were waited for; matrix products, arithmetic and copies ran while one was open for 2% of the time, Pallas kernels for 0%

profile of v8, /device:TPU:1, one launch (start us, length us, event | category | flops | bytes accessed | tf_op | source)
XLA Modules:
  0.0 120.7 jit_solution(5492617845452411903)
XLA Ops:
  0.6 0.0 copy-start.2
  0.6 0.0 copy-start
  0.7 0.6 copy-done.2
  1.4 0.0 copy-done
  1.4 0.1 fusion
  1.5 0.1 select_n.44
  1.6 0.1 copy.14
  1.7 0.1 select_n.47
  1.8 0.1 copy.15
  1.9 0.1 pad_maximum_fusion
  2.0 4.0 %collective-permute-start = (bf16[48,128]{1,0:T(8,128)(2,1)S(1)}, bf16[48,128]{1,0:T(8,128)(2,1)S(1)}, u32[]{:S(2)}, u32[]{:S(2)}) collective-permute-start(bf16[48,128]{1,0:T(8,128)(2,1)S(1)} %pad_maximum_fusion), channel_id=1, source_target_pairs={{0,1},{1,2},{2,3},{3,4},{4,5},{5,6},{6,7},{7,8},{8,9},{9,10},{10,1... | collective-permute-start | bytes 36872 | tf_op jit(solution)/shard_map/ppermute | solution.py:228
  5.9 0.0 copy-start.1
  6.6 0.0 copy-done.1
  6.6 0.1 broadcast_select_fusion.2.extra_ref
  6.7 0.0 copy-start.3
  6.7 0.0 copy-start.4
  6.7 0.6 copy-done.3
  7.4 0.0 copy-done.4
  7.4 2.1 %reshape.39.tangent_ref = bf16[64,64,64]{2,1,0:T(8,128)(2,1)S(1)} reshape(bf16[1,1,64,4096]{3,2,1,0:T(8,128)(2,1)} %param.7) | data formatting | bytes 1048576 | tf_op jit(solution)/shard_map/reshape | solution.py:235
  9.4 14.6 %collective-permute-done.basis_ref = bf16[48,128]{1,0:T(8,128)(2,1)S(1)} collective-permute-done((bf16[48,128]{1,0:T(8,128)(2,1)S(1)}, bf16[48,128]{1,0:T(8,128)(2,1)S(1)}, u32[]{:S(2)}, u32[]{:S(2)}) %collective-permute-start) | collective-permute-done | bytes 12320 | tf_op jit(solution)/shard_map/ppermute | solution.py:228
  24.0 18.8 %all_to_all.30.basis_ref = bf16[16,48,128]{2,1,0:T(8,128)(2,1)S(1)} all-to-all(bf16[16,48,128]{2,1,0:T(8,128)(2,1)S(1)} %broadcast_in_dim.43), channel_id=1, replica_groups=mesh['y'=8,'core'=2,'z_hi'=8,'z_lo'=2,'x'=4] {'y','core'}, dimensions={0} | all-to-all | bytes 393216 | tf_op jit(solution)/shard_map/all_to_all | solution.py:237
  42.8 2.2 %shard_map.94 = s32[64,32,128]{2,1,0:T(8,128)S(1)} custom-call(s32[64]{0:T(128)S(1)} %bitcast_add_fusion.slot_ref, bf16[64,64,64]{2,1,0:T(8,128)(2,1)S(1)} %reshape.39.tangent_ref, bf16[16,48,128]{2,1,0:T(8,128)(2,1)S(1)} %all_to_all.30.basis_ref), custom_call_target="tpu_custom_call" | custom-call | tf_op jit(solution)/shard_map/pallas_call | solution.py:238
  45.1 18.0 %all_to_all.31 = s32[64,32,128]{2,1,0:T(8,128)S(1)} all-to-all(s32[64,32,128]{2,1,0:T(8,128)S(1)} %shard_map.94), channel_id=1, replica_groups=mesh['y'=8,'core'=2,'z_hi'=8,'z_lo'=2,'x'=4] {'z_lo','x'}, dimensions={0} | all-to-all | bytes 2097152 | tf_op jit(solution)/shard_map/all_to_all | solution.py:246
  63.0 0.8 shard_map.95
  63.9 17.4 %all_to_all.32.far_ref = s32[8,32,128]{2,1,0:T(8,128)S(1)} all-to-all(s32[8,32,128]{2,1,0:T(8,128)S(1)} %shard_map.95), channel_id=1, replica_groups=mesh['y'=8,'core'=2,'z_hi'=8,'z_lo'=2,'x'=4] {'z_hi'}, dimensions={0} | all-to-all | bytes 262144 | tf_op jit(solution)/shard_map/all_to_all | solution.py:255
  81.2 0.8 shard_map.96
  82.1 12.2 %all_to_all.33 = f32[8,4,384]{2,1,0:T(4,128)S(1)} all-to-all(f32[8,4,384]{2,1,0:T(4,128)S(1)} %broadcast_in_dim.44), channel_id=1, replica_groups=mesh['y'=8,'core'=2,'z_hi'=8,'z_lo'=2,'x'=4] {'core','x'}, dimensions={0} | all-to-all | bytes 98304 | tf_op jit(solution)/shard_map/all_to_all | solution.py:218
  94.3 14.5 %all_to_all.34 = f32[16,4,384]{2,1,0:T(4,128)S(1)} all-to-all(f32[16,4,384]{2,1,0:T(4,128)S(1)} %broadcast_in_dim.45), channel_id=1, replica_groups=mesh['y'=8,'core'=2,'z_hi'=8,'z_lo'=2,'x'=4] {'z_hi','z_lo'}, dimensions={0} | all-to-all | bytes 196608 | tf_op jit(solution)/shard_map/all_to_all | solution.py:218
  108.8 9.4 %all_to_all.35 = f32[8,4,384]{2,1,0:T(4,128)S(1)} all-to-all(f32[8,4,384]{2,1,0:T(4,128)S(1)} %broadcast_in_dim.46), channel_id=1, replica_groups=mesh['y'=8,'core'=2,'z_hi'=8,'z_lo'=2,'x'=4] {'y'}, dimensions={0} | all-to-all | bytes 98304 | tf_op jit(solution)/shard_map/all_to_all | solution.py:218
  118.3 2.4 %shard_map.97 = (bf16[2,3072]{1,0:T(2,128)(2,1)}, bf16[2,3072]{1,0:T(2,128)(2,1)}, f32[48]{0:T(128)}) custom-call(f32[4,384]{1,0:T(4,128)S(1)} %reduce_sum.29.gram_ref, f32[48,128]{1,0:T(8,128)S(1)} %get-tuple-element.14.product_ref, bf16[48,128]{1,0:T(8,128)(2,1)S(1)} %collective-permute-done.basis_ref), custom_call_target="tpu_custom_call" | custom-call | tf_op jit(solution)/shard_map/pallas_call | solution.py:269
  (9 shorter events, 0.2 us)
Async XLA Ops:
  0.6 0.7 copy-start.2
  0.6 0.8 copy-start
  2.0 22.0 %collective-permute-start = (bf16[48,128]{1,0:T(8,128)(2,1)S(1)}, bf16[48,128]{1,0:T(8,128)(2,1)S(1)}, u32[]{:S(2)}, u32[]{:S(2)}) collective-permute-start(bf16[48,128]{1,0:T(8,128)(2,1)S(1)} %pad_maximum_fusion), channel_id=1, source_target_pairs={{0,1},{1,2},{2,3},{3,4},{4,5},{5,6},{6,7},{7,8},{8,9},{9,10},{10,1... | collective-permute-start | bytes 36872 | tf_op jit(solution)/shard_map/ppermute | solution.py:228
  5.9 0.7 copy-start.1
  6.7 0.7 copy-start.3
  6.7 0.7 copy-start.4

commit v9 on v8

--- a/solution.py
+++ b/solution.py
@@ -229,12 +229,12 @@
     rows, cols = block_row.reshape(NNZ), block_col.reshape(NNZ)
     owner = rows >> 1
     side = jnp.where(jnp.arange(NNZ) < tile_count.reshape(1), rows & 1, 2)
-    slots = (owner & (N_NEAR - 1)) * N_Z_HI + (owner >> 3) + (side << 6) + (cols << 8)
+    slots = (owner & (N_NEAR - 1)) * N_Z_HI + (owner >> 3) + (side << 6) + ((((cols >> 1) & 1) * 2 * N_Y + (cols >> 2) * 2 + (cols & 1)) << 8)
     at_row = lax.broadcasted_iota(jnp.int32, (PAIR - K, PAIR), 0)
     extra = jnp.where(at_row == K, residual.reshape(1, PAIR), 0.0)
     blocks, slots, extra, sent = lax.optimization_barrier((tangent.reshape(NNZ, BLK, BLK), slots, extra, placed))
     copies = jnp.broadcast_to(sent[None], (N_ROW, K, PAIR))
-    col_basis = lax.all_to_all(copies, ROW, 0, 0, tiled=True)
+    col_basis = lax.all_to_all(copies, ("core", "y"), 0, 0, tiled=True)
     partial = pl.pallas_call(
         product_kernel,
         out_shape=jax.ShapeDtypeStruct((N_COL, WORDS, PAIR), jnp.int32),

time: 122 us -> 122 us (level)
    all_to_all x3, blocking collectives: 36.1 us -> 38.4 us  [summed(): return jnp.sum(lax.all_to_all(copies, axes, 0, 0, tiled=True), axis=0)]
    all_to_all x1, blocking collectives: 18.8 us -> 16.7 us  [per_device(): col_basis = lax.all_to_all(copies, ('core', 'y'), 0, 0, tiled=True)]
    all_to_all x1, blocking collectives: 18 us -> 16.7 us  [per_device(): near = lax.all_to_all(partial, NEAR, 0, 0, tiled=True)]
where the time goes in v9:
time: 122 us; the launch traced here: 120 us
  blocking collectives  89.6 us (73%)
  waiting for transfers between devices  14.6 us (12%)
  Pallas kernels  6.33 us (5%)
  starting transfers between devices  3.95 us (3%)
  local copies, waits for them, and re-layouts  3.79 us (3%)
  between operations  1.55 us (1%)
    all_to_all x3, blocking collectives, summed(): return jnp.sum(lax.all_to_all(copies, axes, 0, 0, tiled=True), axis=0)  38.4 us
    all_to_all x1, blocking collectives, per_device(): far = lax.all_to_all(near, 'z_hi', 0, 0, tiled=True)  17.8 us
    all_to_all x1, blocking collectives, per_device(): col_basis = lax.all_to_all(copies, ('core', 'y'), 0, 0, tiled=True)  16.7 us
    all_to_all x1, blocking collectives, per_device(): near = lax.all_to_all(partial, NEAR, 0, 0, tiled=True)  16.7 us
    ppermute x1, waiting for transfers between devices, per_device(): lax.ppermute(sideways, COL, [(i, (i + 1) % N_COL) for i in range(N_COL)])  14.6 us
    ppermute x1, starting transfers between devices, per_device(): lax.ppermute(sideways, COL, [(i, (i + 1) % N_COL) for i in range(N_COL)])  3.95 us
    pallas_call x1, Pallas kernels, per_device(): pl.pallas_call(finish_kernel, out_shape=(jax.ShapeDtypeStruct((2, BLK * K...  2.44 us
  transfers between devices with their start and end apart: 1, of which 1 were waited for; matrix products, arithmetic and copies ran while one was open for 2% of the time, Pallas kernels for 0%

profile of v9, /device:TPU:1, one launch (start us, length us, event | category | flops | bytes accessed | tf_op | source)
XLA Modules:
  0.0 120.1 jit_solution(13966962111863225037)
XLA Ops:
  0.6 0.0 copy-start.2
  0.6 0.0 copy-start
  0.7 0.6 copy-done.2
  1.4 0.0 copy-done
  1.4 0.1 fusion
  1.5 0.1 select_n.44
  1.6 0.1 copy.14
  1.7 0.1 select_n.47
  1.8 0.1 copy.15
  1.9 0.1 pad_maximum_fusion
  2.0 4.0 %collective-permute-start = (bf16[48,128]{1,0:T(8,128)(2,1)S(1)}, bf16[48,128]{1,0:T(8,128)(2,1)S(1)}, u32[]{:S(2)}, u32[]{:S(2)}) collective-permute-start(bf16[48,128]{1,0:T(8,128)(2,1)S(1)} %pad_maximum_fusion), channel_id=1, source_target_pairs={{0,1},{1,2},{2,3},{3,4},{4,5},{5,6},{6,7},{7,8},{8,9},{9,10},{10,1... | collective-permute-start | bytes 36872 | tf_op jit(solution)/shard_map/ppermute | solution.py:228
  5.9 0.0 copy-start.1
  6.6 0.0 copy-done.1
  6.6 0.1 broadcast_select_fusion.2.extra_ref
  6.7 0.0 copy-start.3
  6.7 0.0 copy-start.4
  6.7 0.6 copy-done.3
  7.4 0.0 copy-done.4
  7.4 2.1 %reshape.50.tangent_ref = bf16[64,64,64]{2,1,0:T(8,128)(2,1)S(1)} reshape(bf16[1,1,64,4096]{3,2,1,0:T(8,128)(2,1)} %param.7) | data formatting | bytes 1048576 | tf_op jit(solution)/shard_map/reshape | solution.py:235
  9.4 14.6 %collective-permute-done.basis_ref = bf16[48,128]{1,0:T(8,128)(2,1)S(1)} collective-permute-done((bf16[48,128]{1,0:T(8,128)(2,1)S(1)}, bf16[48,128]{1,0:T(8,128)(2,1)S(1)}, u32[]{:S(2)}, u32[]{:S(2)}) %collective-permute-start) | collective-permute-done | bytes 12320 | tf_op jit(solution)/shard_map/ppermute | solution.py:228
  24.0 16.7 %all_to_all.30.basis_ref = bf16[16,48,128]{2,1,0:T(8,128)(2,1)S(1)} all-to-all(bf16[16,48,128]{2,1,0:T(8,128)(2,1)S(1)} %broadcast_in_dim.46), channel_id=1, replica_groups=mesh['y'=8,'core'=2,'z_hi'=8,'z_lo'=2,'x'=4] {'core','y'}, dimensions={0} | all-to-all | bytes 393216 | tf_op jit(solution)/shard_map/all_to_all | solution.py:237
  40.8 2.2 %shard_map.94 = s32[64,32,128]{2,1,0:T(8,128)S(1)} custom-call(s32[64]{0:T(128)S(1)} %bitcast_add_fusion.slot_ref, bf16[64,64,64]{2,1,0:T(8,128)(2,1)S(1)} %reshape.50.tangent_ref, bf16[16,48,128]{2,1,0:T(8,128)(2,1)S(1)} %all_to_all.30.basis_ref), custom_call_target="tpu_custom_call" | custom-call | tf_op jit(solution)/shard_map/pallas_call | solution.py:238
  43.0 16.7 %all_to_all.31 = s32[64,32,128]{2,1,0:T(8,128)S(1)} all-to-all(s32[64,32,128]{2,1,0:T(8,128)S(1)} %shard_map.94), channel_id=1, replica_groups=mesh['y'=8,'core'=2,'z_hi'=8,'z_lo'=2,'x'=4] {'z_lo','x'}, dimensions={0} | all-to-all | bytes 2097152 | tf_op jit(solution)/shard_map/all_to_all | solution.py:246
  59.7 0.8 shard_map.95
  60.5 17.8 %all_to_all.32.far_ref = s32[8,32,128]{2,1,0:T(8,128)S(1)} all-to-all(s32[8,32,128]{2,1,0:T(8,128)S(1)} %shard_map.95), channel_id=1, replica_groups=mesh['y'=8,'core'=2,'z_hi'=8,'z_lo'=2,'x'=4] {'z_hi'}, dimensions={0} | all-to-all | bytes 262144 | tf_op jit(solution)/shard_map/all_to_all | solution.py:255
  78.3 0.8 shard_map.96
  79.1 11.7 %all_to_all.33 = f32[8,4,384]{2,1,0:T(4,128)S(1)} all-to-all(f32[8,4,384]{2,1,0:T(4,128)S(1)} %broadcast_in_dim.47), channel_id=1, replica_groups=mesh['y'=8,'core'=2,'z_hi'=8,'z_lo'=2,'x'=4] {'core','x'}, dimensions={0} | all-to-all | bytes 98304 | tf_op jit(solution)/shard_map/all_to_all | solution.py:218
  90.9 14.4 %all_to_all.34 = f32[16,4,384]{2,1,0:T(4,128)S(1)} all-to-all(f32[16,4,384]{2,1,0:T(4,128)S(1)} %broadcast_in_dim.48), channel_id=1, replica_groups=mesh['y'=8,'core'=2,'z_hi'=8,'z_lo'=2,'x'=4] {'z_hi','z_lo'}, dimensions={0} | all-to-all | bytes 196608 | tf_op jit(solution)/shard_map/all_to_all | solution.py:218
  105.3 12.3 %all_to_all.35 = f32[8,4,384]{2,1,0:T(4,128)S(1)} all-to-all(f32[8,4,384]{2,1,0:T(4,128)S(1)} %broadcast_in_dim.49), channel_id=1, replica_groups=mesh['y'=8,'core'=2,'z_hi'=8,'z_lo'=2,'x'=4] {'y'}, dimensions={0} | all-to-all | bytes 98304 | tf_op jit(solution)/shard_map/all_to_all | solution.py:218
  117.6 2.4 %shard_map.97 = (bf16[2,3072]{1,0:T(2,128)(2,1)}, bf16[2,3072]{1,0:T(2,128)(2,1)}, f32[48]{0:T(128)}) custom-call(f32[4,384]{1,0:T(4,128)S(1)} %reduce_sum.29.gram_ref, f32[48,128]{1,0:T(8,128)S(1)} %get-tuple-element.14.product_ref, bf16[48,128]{1,0:T(8,128)(2,1)S(1)} %collective-permute-done.basis_ref), custom_call_target="tpu_custom_call" | custom-call | tf_op jit(solution)/shard_map/pallas_call | solution.py:269
  (9 shorter events, 0.2 us)
Async XLA Ops:
  0.6 0.7 copy-start.2
  0.6 0.8 copy-start
  2.0 22.0 %collective-permute-start = (bf16[48,128]{1,0:T(8,128)(2,1)S(1)}, bf16[48,128]{1,0:T(8,128)(2,1)S(1)}, u32[]{:S(2)}, u32[]{:S(2)}) collective-permute-start(bf16[48,128]{1,0:T(8,128)(2,1)S(1)} %pad_maximum_fusion), channel_id=1, source_target_pairs={{0,1},{1,2},{2,3},{3,4},{4,5},{5,6},{6,7},{7,8},{8,9},{9,10},{10,1... | collective-permute-start | bytes 36872 | tf_op jit(solution)/shard_map/ppermute | solution.py:228
  5.9 0.7 copy-start.1
  6.7 0.7 copy-start.3
  6.7 0.7 copy-start.4
